TPU v7x, 32 devices: a whole 2x2x4 slice. The times are simulated.
32 devices in a mesh: lat: 8 (over y, x, core), blk: 4 (over z).
Axes of the slice: x: 2, y: 2, z: 4, core: 2. Of those that a mesh axis runs over, the one named last changes fastest.
Arguments:
- tokens: float32 [8, 1024, 1152], P('lat', 'blk'), may hold values from -6 to 6
- condition: float32 [8, 1152], P('lat'), may hold values from -6 to 6
- cotangent: float32 [8, 1024, 1152], P('lat', 'blk'), may hold values from -6 to 6
- ada_weight: float32 [1152, 6912], P(('lat', 'blk')), may hold values from -0.1875 to 0.1875
- ada_bias: float32 [6912], P(('lat', 'blk')), may hold values from -2 to 2
- qkv_weight: float32 [1152, 3456], P(('lat', 'blk')), may hold values from -0.1875 to 0.1875
- query_bias: float32 [1152], P(('lat', 'blk')), may hold values from -3 to 3
- value_bias: float32 [1152], P(('lat', 'blk')), may hold values from -0.6 to 0.6
- proj_weight: float32 [1152, 1152], P(('lat', 'blk')), may hold values from -6 to 6
- proj_bias: float32 [1152], P(('lat', 'blk')), may hold values from -3 to 3
- up_weight: float32 [1152, 4608], P(('lat', 'blk')), may hold values from -0.1875 to 0.1875
- up_bias: float32 [4608], P(('lat', 'blk')), may hold values from -3 to 3
- down_weight: float32 [4608, 1152], P(('lat', 'blk')), may hold values from -0.09375 to 0.09375
- down_bias: float32 [1152], P(('lat', 'blk')), may hold values from -3 to 3
Outputs:
- output: float32 [8, 1024, 1152], P('lat', 'blk')
- grad_tokens: float32 [8, 1024, 1152], P('lat', 'blk')
- grad_condition: float32 [8, 1152], P('lat')
- grad_ada_weight: float32 [1152, 6912], P(('lat', 'blk'))
- grad_ada_bias: float32 [6912], P(('lat', 'blk'))
- grad_qkv_weight: float32 [1152, 3456], P(('lat', 'blk'))
- grad_query_bias: float32 [1152], P(('lat', 'blk'))
- grad_value_bias: float32 [1152], P(('lat', 'blk'))
- grad_proj_weight: float32 [1152, 1152], P(('lat', 'blk'))
- grad_proj_bias: float32 [1152], P(('lat', 'blk'))
- grad_up_weight: float32 [1152, 4608], P(('lat', 'blk'))
- grad_up_bias: float32 [4608], P(('lat', 'blk'))
- grad_down_weight: float32 [4608, 1152], P(('lat', 'blk'))
- grad_down_bias: float32 [1152], P(('lat', 'blk'))
All inputs are finite; a program needn't handle non-finite values.
Results may differ from a plain program's by a relative error of at most 0.018.
The roundings to bfloat16 on the way count: a program that leaves them out, or rounds other values in their place, can miss the bound.
Values may be sent and summed in bfloat16 or wider, within the bound.
A program may use at most 320 MiB of HBM per device.

v0:
```python
import math

import jax
import jax.numpy as jnp
from jax import lax
from jax.sharding import PartitionSpec as P

H = 16


EPS = 1e-06
GELU_C = 0.7978845608028654
CUBIC = 0.044715
HIGH = lax.Precision.HIGHEST


def layer_norm(value):
    mean = jnp.mean(value, axis=-1, keepdims=True)
    centered = value - mean
    rstd = lax.rsqrt(jnp.mean(centered * centered, axis=-1, keepdims=True) + EPS)
    return (centered * rstd, rstd)


def norm_back(grad, normed, rstd):
    return (
        grad
        - jnp.mean(grad, axis=-1, keepdims=True)
        - normed * jnp.mean(grad * normed, axis=-1, keepdims=True)
    ) * rstd


def gelu_tanh(value):
    return 0.5 * value * (1.0 + jnp.tanh(GELU_C * (value + CUBIC * value * value * value)))


def gelu_slope(value):
    inner = jnp.tanh(GELU_C * (value + CUBIC * value * value * value))
    return 0.5 * (1.0 + inner) + 0.5 * value * (1.0 - inner * inner) * GELU_C * (
        1.0 + 3.0 * CUBIC * value * value
    )


def silu_slope(value):
    sigma = jax.nn.sigmoid(value)
    return sigma * (1.0 + value * (1.0 - sigma))


def flatten(array):
    return array.reshape(-1, array.shape[-1])


def weight_term(left, right):
    return jnp.einsum(
        "nd,nf->df", flatten(left), flatten(right), preferred_element_type=jnp.float32
    )


def token_sum(array):
    return jnp.sum(array, axis=1)


def per_device(
    tokens,
    condition,
    cotangent,
    ada_weight,
    ada_bias,
    qkv_weight,
    query_bias,
    value_bias,
    proj_weight,
    proj_bias,
    up_weight,
    up_bias,
    down_weight,
    down_bias,
):
    lat_dev, rows, width = tokens.shape
    heads = H
    head_size = width // heads
    scale = 1.0 / math.sqrt(head_size)
    blk_size = lax.axis_size("blk")
    lat_size = lax.axis_size("lat")
    first_local = (
        ada_weight.astype(jnp.bfloat16),
        ada_bias.astype(jnp.bfloat16),
        qkv_weight.astype(jnp.bfloat16),
        query_bias.astype(jnp.bfloat16),
        value_bias.astype(jnp.bfloat16),
        proj_weight.astype(jnp.bfloat16),
        proj_bias.astype(jnp.bfloat16),
    )
    second_local = (
        up_weight.astype(jnp.bfloat16),
        up_bias.astype(jnp.bfloat16),
        down_weight.astype(jnp.bfloat16),
        down_bias.astype(jnp.bfloat16),
    )
    mod_matrix, mod_offset, qkv_matrix, query_offset, value_offset, out_matrix, out_offset = (
        lax.all_gather(first_local[0], ("lat", "blk"), axis=0, tiled=True),
        lax.all_gather(first_local[1], ("lat", "blk"), axis=0, tiled=True),
        lax.all_gather(first_local[2], ("lat", "blk"), axis=0, tiled=True),
        lax.all_gather(first_local[3], ("lat", "blk"), axis=0, tiled=True),
        lax.all_gather(first_local[4], ("lat", "blk"), axis=0, tiled=True),
        lax.all_gather(first_local[5], ("lat", "blk"), axis=0, tiled=True),
        lax.all_gather(first_local[6], ("lat", "blk"), axis=0, tiled=True),
    )
    cond_act = jax.nn.silu(condition)
    modulation = jnp.dot(
        cond_act.astype(jnp.bfloat16), mod_matrix, preferred_element_type=jnp.float32
    ) + mod_offset.astype(jnp.float32)
    shift1, scale1, gate1, shift2, scale2, gate2 = [
        piece[:, None, :] for piece in jnp.split(modulation, 6, axis=1)
    ]
    normed1, rstd1 = layer_norm(tokens)
    attn_in = (normed1 * (1.0 + scale1) + shift1).astype(jnp.bfloat16)
    offsets = jnp.concatenate([query_offset, jnp.zeros_like(query_offset), value_offset]).astype(
        jnp.float32
    )
    qkv = (jnp.dot(attn_in, qkv_matrix, preferred_element_type=jnp.float32) + offsets).astype(
        jnp.bfloat16
    )
    query = qkv[..., :width].reshape(lat_dev, rows, heads, head_size)
    keys = qkv[..., width : 2 * width]
    values = qkv[..., 2 * width :]
    pieces = (
        lax.all_gather(keys, "blk", axis=1, tiled=True),
        lax.all_gather(values, "blk", axis=1, tiled=True),
    )
    peak = jnp.full((lat_dev, heads, rows), -1e30, jnp.float32)
    key_piece = pieces[0].reshape(lat_dev, -1, heads, head_size)
    value_piece = pieces[1].reshape(lat_dev, -1, heads, head_size)
    scores = (
        jnp.einsum("bqhd,bkhd->bhqk", query, key_piece, preferred_element_type=jnp.float32) * scale
    )
    fresh = jnp.maximum(peak, jnp.max(scores, axis=-1))
    expo = jnp.exp(scores - fresh[..., None])
    total = jnp.sum(expo, axis=-1)
    accum = jnp.einsum(
        "bhqk,bkhd->bhqd",
        expo.astype(jnp.bfloat16),
        value_piece,
        preferred_element_type=jnp.float32,
    )
    peak, total, accum = (fresh, total, accum)
    log_total = peak + jnp.log(total)
    attn4 = (accum / total[..., None]).transpose(0, 2, 1, 3).astype(jnp.bfloat16)
    attn = attn4.reshape(lat_dev, rows, width)
    proj = jnp.dot(attn, out_matrix, preferred_element_type=jnp.float32) + out_offset.astype(
        jnp.float32
    )
    mid = tokens + gate1 * proj
    normed2, rstd2 = layer_norm(mid)
    mlp_in = (normed2 * (1.0 + scale2) + shift2).astype(jnp.bfloat16)
    up_matrix, up_offset, down_matrix, down_offset = (
        lax.all_gather(second_local[0], ("lat", "blk"), axis=0, tiled=True),
        lax.all_gather(second_local[1], ("lat", "blk"), axis=0, tiled=True),
        lax.all_gather(second_local[2], ("lat", "blk"), axis=0, tiled=True),
        lax.all_gather(second_local[3], ("lat", "blk"), axis=0, tiled=True),
    )
    hidden = jnp.dot(mlp_in, up_matrix, preferred_element_type=jnp.float32) + up_offset.astype(
        jnp.float32
    )
    act = gelu_tanh(hidden).astype(jnp.bfloat16)
    mlp_out = jnp.dot(act, down_matrix, preferred_element_type=jnp.float32) + down_offset.astype(
        jnp.float32
    )
    output = mid + gate2 * mlp_out
    up_matrix, up_offset, down_matrix, down_offset = (
        lax.all_gather(second_local[0], ("lat", "blk"), axis=0, tiled=True),
        lax.all_gather(second_local[1], ("lat", "blk"), axis=0, tiled=True),
        lax.all_gather(second_local[2], ("lat", "blk"), axis=0, tiled=True),
        lax.all_gather(second_local[3], ("lat", "blk"), axis=0, tiled=True),
    )
    grad_gate2 = token_sum(cotangent * mlp_out)
    d_mlp = cotangent * gate2
    d_mlp16 = d_mlp.astype(jnp.bfloat16)
    down_term = weight_term(act, d_mlp16)
    down_bias_term = jnp.sum(flatten(d_mlp), axis=0)
    d_hidden = jnp.einsum(
        "btd,fd->btf", d_mlp16, down_matrix, preferred_element_type=jnp.float32
    ) * gelu_slope(hidden)
    d_hidden16 = d_hidden.astype(jnp.bfloat16)
    up_term = weight_term(mlp_in, d_hidden16)
    up_bias_term = jnp.sum(flatten(d_hidden), axis=0)
    up_grad, up_bias_grad, down_grad, down_bias_grad = (
        lax.psum_scatter(up_term, ("lat", "blk"), scatter_dimension=0, tiled=True),
        lax.psum_scatter(up_bias_term, ("lat", "blk"), scatter_dimension=0, tiled=True),
        lax.psum_scatter(down_term, ("lat", "blk"), scatter_dimension=0, tiled=True),
        lax.psum_scatter(down_bias_term, ("lat", "blk"), scatter_dimension=0, tiled=True),
    )
    d_mlp_in = jnp.einsum("btf,df->btd", d_hidden16, up_matrix, preferred_element_type=jnp.float32)
    grad_shift2 = token_sum(d_mlp_in)
    grad_scale2 = token_sum(d_mlp_in * normed2)
    d_mid = cotangent + norm_back(d_mlp_in * (1.0 + scale2), normed2, rstd2)
    mod_matrix, mod_offset, qkv_matrix, query_offset, value_offset, out_matrix, out_offset = (
        lax.all_gather(first_local[0], ("lat", "blk"), axis=0, tiled=True),
        lax.all_gather(first_local[1], ("lat", "blk"), axis=0, tiled=True),
        lax.all_gather(first_local[2], ("lat", "blk"), axis=0, tiled=True),
        lax.all_gather(first_local[3], ("lat", "blk"), axis=0, tiled=True),
        lax.all_gather(first_local[4], ("lat", "blk"), axis=0, tiled=True),
        lax.all_gather(first_local[5], ("lat", "blk"), axis=0, tiled=True),
        lax.all_gather(first_local[6], ("lat", "blk"), axis=0, tiled=True),
    )
    grad_gate1 = token_sum(d_mid * proj)
    d_proj = d_mid * gate1
    d_proj16 = d_proj.astype(jnp.bfloat16)
    proj_term = weight_term(attn, d_proj16)
    proj_bias_term = jnp.sum(flatten(d_proj), axis=0)
    d_attn = jnp.einsum(
        "btd,ed->bte", d_proj16, out_matrix, preferred_element_type=jnp.float32
    ).astype(jnp.bfloat16)
    d_attn4 = d_attn.reshape(lat_dev, rows, heads, head_size)
    delta = jnp.einsum("bqhd,bqhd->bhq", d_attn4, attn4, preferred_element_type=jnp.float32)
    pieces = (
        lax.all_gather(keys, "blk", axis=1, tiled=True),
        lax.all_gather(values, "blk", axis=1, tiled=True),
    )
    key_flat = pieces[0]
    count = key_flat.shape[1]
    key_piece = key_flat.reshape(lat_dev, count, heads, head_size)
    value_piece = pieces[1].reshape(lat_dev, count, heads, head_size)
    scores = (
        jnp.einsum("bqhd,bkhd->bhqk", query, key_piece, preferred_element_type=jnp.float32) * scale
    )
    probs = jnp.exp(scores - log_total[..., None])
    value_part = jnp.einsum(
        "bhqk,bqhd->bkhd", probs.astype(jnp.bfloat16), d_attn4, preferred_element_type=jnp.float32
    )
    d_probs = jnp.einsum(
        "bqhd,bkhd->bhqk", d_attn4, value_piece, preferred_element_type=jnp.float32
    )
    d_scores = (probs * (d_probs - delta[..., None]) * scale).astype(jnp.bfloat16)
    query_part = jnp.einsum(
        "bhqk,bkhd->bqhd", d_scores, key_piece, preferred_element_type=jnp.float32
    )
    key_part = jnp.einsum("bhqk,bqhd->bkhd", d_scores, query, preferred_element_type=jnp.float32)
    query_part, key_part, value_part = (
        query_part,
        key_part.reshape(lat_dev, count, width),
        value_part.reshape(lat_dev, count, width),
    )
    grad_query = query_part
    grad_keys = key_part
    grad_values = value_part
    grad_query, grad_keys, grad_values = (grad_query, grad_keys, grad_values)
    key_grad, value_grad = (
        lax.psum_scatter(grad_keys, "blk", scatter_dimension=1, tiled=True),
        lax.psum_scatter(grad_values, "blk", scatter_dimension=1, tiled=True),
    )
    query_grad = grad_query.reshape(lat_dev, rows, width)
    d_qkv = jnp.concatenate([query_grad, key_grad, value_grad], axis=-1).astype(jnp.bfloat16)
    qkv_term = weight_term(attn_in, d_qkv)
    query_bias_term = jnp.sum(flatten(query_grad), axis=0)
    value_bias_term = jnp.sum(flatten(value_grad), axis=0)
    d_attn_in = jnp.einsum("btc,dc->btd", d_qkv, qkv_matrix, preferred_element_type=jnp.float32)
    grad_shift1 = token_sum(d_attn_in)
    grad_scale1 = token_sum(d_attn_in * normed1)
    grad_tokens = d_mid + norm_back(d_attn_in * (1.0 + scale1), normed1, rstd1)
    d_mod_local = jnp.concatenate(
        [grad_shift1, grad_scale1, grad_gate1, grad_shift2, grad_scale2, grad_gate2], axis=1
    )
    d_mod = lax.psum(d_mod_local, "blk")
    grad_condition = jnp.einsum(
        "bj,dj->bd", d_mod, mod_matrix.astype(jnp.float32), precision=HIGH
    ) * silu_slope(condition)
    share_rows = width // (lat_size * blk_size)
    picked = lax.dynamic_index_in_dim(
        cond_act.reshape(lat_dev, lat_size, blk_size, share_rows),
        lax.axis_index("blk"),
        axis=2,
        keepdims=False,
    )
    ada_term = jnp.einsum("blr,bc->lrc", picked, d_mod, precision=HIGH)
    mod_total = jnp.sum(d_mod, axis=0)
    offset_rows = mod_total.shape[0] // (lat_size * blk_size)
    ada_bias_term = lax.dynamic_index_in_dim(
        mod_total.reshape(lat_size, blk_size, offset_rows),
        lax.axis_index("blk"),
        axis=1,
        keepdims=False,
    )
    ada_grad, ada_bias_grad = (
        lax.psum_scatter(ada_term, "lat", scatter_dimension=0, tiled=True),
        lax.psum_scatter(ada_bias_term, "lat", scatter_dimension=0, tiled=True),
    )
    qkv_grad, query_bias_grad, value_bias_grad, proj_grad, proj_bias_grad = (
        lax.psum_scatter(qkv_term, ("lat", "blk"), scatter_dimension=0, tiled=True),
        lax.psum_scatter(query_bias_term, ("lat", "blk"), scatter_dimension=0, tiled=True),
        lax.psum_scatter(value_bias_term, ("lat", "blk"), scatter_dimension=0, tiled=True),
        lax.psum_scatter(proj_term, ("lat", "blk"), scatter_dimension=0, tiled=True),
        lax.psum_scatter(proj_bias_term, ("lat", "blk"), scatter_dimension=0, tiled=True),
    )
    return (
        output,
        grad_tokens,
        grad_condition,
        ada_grad.reshape(ada_grad.shape[1], ada_grad.shape[2]),
        ada_bias_grad.reshape(-1),
        qkv_grad,
        query_bias_grad,
        value_bias_grad,
        proj_grad,
        proj_bias_grad,
        up_grad,
        up_bias_grad,
        down_grad,
        down_bias_grad,
    )


def solution(mesh):
    in_specs = (
        P("lat", "blk", None),
        P("lat", None),
        P("lat", "blk", None),
        P(("lat", "blk"), None),
        P(("lat", "blk")),
        P(("lat", "blk"), None),
        P(("lat", "blk")),
        P(("lat", "blk")),
        P(("lat", "blk"), None),
        P(("lat", "blk")),
        P(("lat", "blk"), None),
        P(("lat", "blk")),
        P(("lat", "blk"), None),
        P(("lat", "blk")),
    )
    out_specs = (
        P("lat", "blk", None),
        P("lat", "blk", None),
        P("lat", None),
        P(("lat", "blk"), None),
        P(("lat", "blk")),
        P(("lat", "blk"), None),
        P(("lat", "blk")),
        P(("lat", "blk")),
        P(("lat", "blk"), None),
        P(("lat", "blk")),
        P(("lat", "blk"), None),
        P(("lat", "blk")),
        P(("lat", "blk"), None),
        P(("lat", "blk")),
    )
    return jax.shard_map(
        per_device, mesh=mesh, in_specs=in_specs, out_specs=out_specs, check_vma=False
    )
```

profile of v0, /device:TPU:0, one launch (start us, length us, event | category | flops | bytes accessed | tf_op | source)
XLA Modules:
  0.0 2389.7 jit_solution(14976856752509899224)
XLA Ops:
  14.8 43.1 %all-reduce.19 = (bf16[1152]{0:T(1024)(128)(2,1)S(1)}, bf16[1152]{0:T(1024)(128)(2,1)S(1)}, bf16[6912]{0:T(1024)(128)(2,1)S(1)}, bf16[1152]{0:T(1024)(128)(2,1)S...) all-reduce(bf16[1152]{0:T(1024)(128)(2,1)S(1)} %dynamic-update-slic, ...), channel_id=1, replica_groups=mesh['lat'=8,'blk'=4] {'lat','blk'}, use_global_device_ids=true, to_apply=%add.2 | all-reduce | flops 16128 | bytes 64512
  58.3 35.4 %all-gather.20.cloned.1.call-done = bf16[32,36,3456]{2,1,0:T(8,128)(2,1)} async-done(((bf16[1,36,3456]{2,1,0:T(8,128)(2,1)}), bf16[32,36,3456]{2,1,0:T(8,128)(2,1)}) %all-gather.20.cloned.1.call-update) | async-done | bytes 7962640 | tf_op jit(solution)/shard_map/all_gather | solution.py:102
  93.6 12.5 reshape.444
  106.2 108.8 %all-gather.18.cloned.1.call-done = bf16[32,36,6912]{2,1,0:T(8,128)(2,1)} async-done(((bf16[1,36,6912]{2,1,0:T(8,128)(2,1)}), bf16[32,36,6912]{2,1,0:T(8,128)(2,1)}) %all-gather.18.cloned.1.call-update) | async-done | bytes 15925264 | tf_op jit(solution)/shard_map/all_gather | solution.py:100
  214.9 18.4 reshape.442
  233.4 7.9 convolution_reduce_fusion
  249.4 26.0 %all-gather.22.cloned.1.call-done = bf16[32,36,1152]{2,1,0:T(8,128)(2,1)} async-done(((bf16[1,36,1152]{2,1,0:T(8,128)(2,1)}), bf16[32,36,1152]{2,1,0:T(8,128)(2,1)}) %all-gather.22.cloned.1.call-update) | async-done | bytes 2654224 | tf_op jit(solution)/shard_map/all_gather | solution.py:105
  275.4 5.2 reshape.446
  280.6 89.1 %all-gather.24.cloned.1.call-done = bf16[32,36,4608]{2,1,0:T(8,128)(2,1)} async-done(((bf16[1,36,4608]{2,1,0:T(8,128)(2,1)}), bf16[32,36,4608]{2,1,0:T(8,128)(2,1)}) %all-gather.24.cloned.1.call-update) | async-done | bytes 10616848 | tf_op jit(solution)/shard_map/all_gather | solution.py:156
  369.7 14.2 reshape.448
  385.0 35.6 %all-gather.14.cloned.1.call-done = bf16[1,1024,1152]{2,1,0:T(8,128)(2,1)} async-done(((bf16[1,256,1152]{2,1,0:T(8,128)(2,1)}), bf16[1,1024,1152]{2,1,0:T(8,128)(2,1)}) %all-gather.14.cloned.1.call-update) | async-done | bytes 2359312 | tf_op jit(solution)/shard_map/all_gather | solution.py:128
  420.5 4.3 copy.46
  424.8 47.1 %all-gather.12.cloned.1.call-done = bf16[1,1024,1152]{2,1,0:T(8,128)(2,1)} async-done(((bf16[1,256,1152]{2,1,0:T(8,128)(2,1)}), bf16[1,1024,1152]{2,1,0:T(8,128)(2,1)}) %all-gather.12.cloned.1.call-update) | async-done | bytes 2359312 | tf_op jit(solution)/shard_map/all_gather | solution.py:127
  485.0 4.5 divide_convert_fusion
  493.7 9.1 convolution_add_fusion
  502.8 58.5 %all-gather.16.cloned.1.call-done = bf16[4608,1152]{1,0:T(8,128)(2,1)} async-done(((bf16[144,1152]{1,0:T(8,128)(2,1)}), bf16[4608,1152]{1,0:T(8,128)(2,1)}) %all-gather.16.cloned.1.call-update) | async-done | bytes 10616848 | tf_op jit(solution)/shard_map/all_gather | solution.py:158
  561.4 9.4 fusion.72
  570.9 8.9 fusion.22
  580.5 9.9 multiply_reduce_fusion.4
  595.5 11.0 fusion.6
  608.0 11.3 multiply_convert_fusion
  619.3 4.3 fusion.73
  628.2 7.5 fusion.71
  635.7 54.7 %reduce-scatter.13.cloned.1.call-done = f32[1,256,1152]{1,2,0:T(8,128)} async-done(((f32[1,1024,1152]{1,2,0:T(8,128)}), f32[1,256,1152]{1,2,0:T(8,128)}) %reduce-scatter.13.cloned.1.call-update) | async-done | bytes 1179664 | tf_op jit(solution)/shard_map/reduce_scatter | solution.py:249
  692.9 85.6 %reduce-scatter.11.cloned.1.call-done = f32[1,256,1152]{1,2,0:T(8,128)} async-done(((f32[1,1024,1152]{1,2,0:T(8,128)}), f32[1,256,1152]{1,2,0:T(8,128)}) %reduce-scatter.11.cloned.1.call-update) | async-done | bytes 1179664 | tf_op jit(solution)/shard_map/reduce_scatter | solution.py:248
  779.9 6.9 fusion.24
  788.7 18.2 psum.7
  807.0 4.1 broadcast_multiply_fusion
  812.4 16.2 fusion.47
  833.4 9.2 fusion.32
  842.7 8.4 fusion.38
  851.1 1201.7 %fusion.66 = (f32[48,3456]{1,0:T(8,128)S(1)}, f32[48,1152]{1,0:T(8,128)S(1)}, f32[40,4608]{1,0:T(8,128)}) fusion(f32[1152,3456]{1,0:T(8,128)} %fusion.38, f32[1152,1152]{1,0:T(8,128)} %fusion.44, f32[1152,4608]{1,0:T(8,128)} %fusion.32), kind=kCustom, calls=%all-reduce-scatter.3 | all-reduce-scatter fusion | flops 12976130 | bytes 44089344
  2059.5 6.8 collective-permute-start.5
  2070.7 30.0 %collective-permute-start.7 = (f32[36,3456]{1,0:T(8,128)S(1)}, f32[36,3456]{1,0:T(8,128)S(1)}, u32[]{:S(2)}, u32[]{:S(2)}) collective-permute-start(f32[36,3456]{1,0:T(8,128)S(1)} %slice.15), channel_id=1, source_target_pairs={{0,8},{1,9},{2,10},{3,11},{4,12},{5,13},{6,14},{7,15},{8,16},{9,17... | collective-permute-start | bytes 1493000
  2100.7 15.8 convolution_multiply_fusion.1
  2116.5 4.7 collective-permute-start.11
  2122.6 4.4 collective-permute-start.9
  2127.0 6.3 collective-permute-start.8
  2133.4 11.9 collective-permute-start.4
  2145.3 7.0 collective-permute-start.3
  2152.3 9.4 collective-permute-start.2
  2168.6 20.7 all-reduce.6
  2189.3 5.2 collective-permute-start.18
  2196.2 3.6 collective-permute-start.16
  2202.0 106.6 %all-reduce.18 = (f32[1152]{0:T(1024)S(1)}, f32[1152]{0:T(1024)S(1)}, f32[1152]{0:T(1024)S(1)}, f32[4608]{0:T(1024)S(1)}, f32[1152]{0:T(1024)S(1)}) all-reduce(f32[1152]{0:T(1024)S(1)} %copy-done.57, f32[1152]{0:T(1024)S(1)} %copy-done.56, f32[1152]{0:T(1024)} %get-tuple-element.57, ...), channel_id=7, replica_groups=mesh['lat'=8,'blk'=4] {'lat','blk'}, use_global_device_ids=true, to_apply=%region_23.24.clone | all-reduce | flops 9216 | bytes 73728
  2311.6 14.8 concatenate.31
  2329.3 36.7 %concatenate.30 = f32[420,3456]{1,0:T(8,128)} concatenate(f32[36,3456]{1,0:T(8,128)} %copy-done.34, f32[48,3456]{1,0:T(8,128)} %copy-done.31, f32[48,3456]{1,0:T(8,128)} %copy-done.32, f32[48,3456]{1,0:T(8,128)} %collective-permute-done.4, f32[48,3456]{1,0:T(8,128)} %collective-permute-done.3, f32[48,3456]{1,0:T(8,128)} %collective-permute-done.2, ...), dimensions={0} | concatenate | bytes 11612160
  2369.7 12.0 concatenate.32
  (312 shorter events, 91.4 us)
Async XLA Ops:
  7.2 86.4 %all-gather.20.cloned.1.call-start = ((), (), s32[]{:S(2)}) async-start(), calls=%async_computation.12 | async-start | bytes 9123840 | tf_op jit(solution)/shard_map/all_gather | solution.py:102
  9.2 205.7 %all-gather.18.cloned.1.call-start = ((), (), s32[]{:S(2)}) async-start(), calls=%async_computation.11 | async-start | bytes 18247680 | tf_op jit(solution)/shard_map/all_gather | solution.py:100
  11.5 263.9 %all-gather.22.cloned.1.call-start = ((), (), s32[]{:S(2)}) async-start(), calls=%async_computation.13 | async-start | bytes 3041280 | tf_op jit(solution)/shard_map/all_gather | solution.py:105
  12.2 357.5 %all-gather.24.cloned.1.call-start = ((), (), s32[]{:S(2)}) async-start(), calls=%async_computation.14 | async-start | bytes 12165120 | tf_op jit(solution)/shard_map/all_gather | solution.py:156
  13.1 407.5 %all-gather.14.cloned.1.call-start = ((), (), s32[]{:S(2)}) async-start(), calls=%async_computation.5 | async-start | bytes 2949120 | tf_op jit(solution)/shard_map/all_gather | solution.py:128
  58.0 184.0 %copy-start.51 = (f32[256]{0:T(256)}, f32[256]{0:T(256)S(1)}, u32[]{:S(2)}) copy-start(f32[256]{0:T(256)S(1)} %broadcast_multiply_fusion.6) | copy-start | bytes 3076
  58.3 183.7 %copy-start.63 = (f32[256]{0:T(256)}, f32[256]{0:T(256)S(1)}, u32[]{:S(2)}) copy-start(f32[256]{0:T(256)S(1)} %add_rsqrt_fusion.1) | copy-start | bytes 3076
  106.2 127.2 %copy-start.49 = (f32[1,1152]{1,0:T(1,128)S(1)}, f32[1,1152]{1,0:T(1,128)}, u32[]{:S(2)}) copy-start(f32[1,1152]{1,0:T(1,128)} %param.15) | copy-start | bytes 13828
  245.9 226.0 %all-gather.12.cloned.1.call-start = ((), (), s32[]{:S(2)}) async-start(), calls=%async_computation.4 | async-start | bytes 2949120 | tf_op jit(solution)/shard_map/all_gather | solution.py:127
  246.5 314.9 %all-gather.16.cloned.1.call-start = ((), (), s32[]{:S(2)}) async-start(), calls=%async_computation.6 | async-start | bytes 10948608 | tf_op jit(solution)/shard_map/all_gather | solution.py:158
  247.3 443.0 %reduce-scatter.13.cloned.1.call-start = ((), (), s32[]{:S(2)}) async-start(), calls=%async_computation.8 | async-start | bytes 5898240 | tf_op jit(solution)/shard_map/reduce_scatter | solution.py:249
  606.5 172.0 %reduce-scatter.11.cloned.1.call-start = ((), (), s32[]{:S(2)}) async-start(), calls=%async_computation.7 | async-start | bytes 5898240 | tf_op jit(solution)/shard_map/reduce_scatter | solution.py:248
  624.1 1758.6 %reduce-scatter.15.cloned.1.call-start = ((), (), s32[]{:S(2)}) async-start(), calls=%async_computation.9 | async-start | bytes 9953280 | tf_op jit(solution)/shard_map/reduce_scatter | solution.py:284
  635.7 144.1 %copy-start.19 = (bf16[1,256,16,72]{1,3,2,0:T(8,128)(2,1)S(1)}, bf16[1,256,16,72]{1,3,2,0:T(8,128)(2,1)}, u32[]{:S(2)}) copy-start(bf16[1,256,16,72]{1,3,2,0:T(8,128)(2,1)} %get-tuple-element.62) | copy-start | bytes 1769476
  635.7 144.1 %copy-start.52 = (f32[256]{0:T(256)S(1)}, f32[256]{0:T(256)}, u32[]{:S(2)}) copy-start(f32[256]{0:T(256)} %copy-done.51) | copy-start | bytes 3076
  635.7 144.1 %copy-start.64 = (f32[256]{0:T(256)S(1)}, f32[256]{0:T(256)}, u32[]{:S(2)}) copy-start(f32[256]{0:T(256)} %copy-done.63) | copy-start | bytes 3076
  692.9 93.9 %copy-start.21 = (bf16[256,1152]{0,1:T(8,128)(2,1)}, bf16[256,1152]{0,1:T(8,128)(2,1)S(1)}, u32[]{:S(2)}) copy-start(bf16[256,1152]{0,1:T(8,128)(2,1)S(1)} %get-tuple-element.60) | copy-start | bytes 1769476
  811.1 1571.6 %reduce-scatter.17.cloned.1.call-start = ((), (), s32[]{:S(2)}) async-start(), calls=%async_computation.10 | async-start | bytes 21897216 | tf_op jit(solution)/shard_map/reduce_scatter | solution.py:189
  851.1 1205.6 %copy-start.85 = (u32[32]{0:T(128)S(1)}, u32[32]{0:T(128)}, u32[]{:S(2)}) copy-start(u32[32]{0:T(128)} %constant.91) | copy-start | bytes 388
  851.1 1206.2 %copy-start.53 = (f32[16,72]{1,0:T(8,128)S(1)}, f32[16,72]{1,0:T(8,128)}, u32[]{:S(2)}) copy-start(f32[16,72]{1,0:T(8,128)} %get-tuple-element.61) | copy-start | bytes 13828
  851.1 1249.6 %copy-start.50 = (f32[1,1152]{1,0:T(1,128)S(1)}, f32[1,1152]{1,0:T(1,128)}, u32[]{:S(2)}) copy-start(f32[1,1152]{1,0:T(1,128)} %param.15) | copy-start | bytes 13828
  2052.8 17.9 collective-permute-start.14
  2054.8 13.5 collective-permute-start.15
  2058.0 75.3 %copy-start.77 = (f32[256]{0:T(256)S(1)}, f32[256]{0:T(256)}, u32[]{:S(2)}) copy-start(f32[256]{0:T(256)} %get-tuple-element.25) | copy-start | bytes 3076
  2058.1 108.9 %copy-start.16 = (f32[256,1152]{1,0:T(8,128)S(1)}, f32[256,1152]{1,0:T(8,128)}, u32[]{:S(2)}) copy-start(f32[256,1152]{1,0:T(8,128)} %copy-done.15) | copy-start | bytes 3538948
  2058.1 108.9 %copy-start.65 = (f32[256]{0:T(256)S(1)}, f32[256]{0:T(256)}, u32[]{:S(2)}) copy-start(f32[256]{0:T(256)} %copy-done.63) | copy-start | bytes 3076
  2058.1 103.6 %collective-permute-start.6 = (f32[48,3456]{1,0:T(8,128)S(1)}, f32[48,3456]{1,0:T(8,128)S(1)}, u32[]{:S(2)}, u32[]{:S(2)}) collective-permute-start(f32[48,3456]{1,0:T(8,128)S(1)} %get-tuple-element.46), channel_id=1, source_target_pairs={{0,7},{1,8},{2,9},{3,10},{4,11},{5,12},{6,13},{7,14},{8,15},{9,16}... | collective-permute-start | bytes 1990664
  2059.5 104.3 %collective-permute-start.5 = (f32[48,3456]{1,0:T(8,128)S(1)}, f32[48,3456]{1,0:T(8,128)S(1)}, u32[]{:S(2)}, u32[]{:S(2)}) collective-permute-start(f32[48,3456]{1,0:T(8,128)S(1)} %get-tuple-element.46), channel_id=1, source_target_pairs={{0,6},{1,7},{2,8},{3,9},{4,10},{5,11},{6,12},{7,13},{8,14},{9,15},... | collective-permute-start | bytes 1990664
  2066.4 50.1 %collective-permute-start.13 = (f32[48,1152]{1,0:T(8,128)S(1)}, f32[48,1152]{1,0:T(8,128)S(1)}, u32[]{:S(2)}, u32[]{:S(2)}) collective-permute-start(f32[48,1152]{1,0:T(8,128)S(1)} %get-tuple-element.47), channel_id=1, source_target_pairs={{0,6},{1,7},{2,8},{3,9},{4,10},{5,11},{6,12},{7,13},{8,14},{9,15},... | collective-permute-start | bytes 663560
  2068.3 52.9 %collective-permute-start.12 = (f32[48,1152]{1,0:T(8,128)S(1)}, f32[48,1152]{1,0:T(8,128)S(1)}, u32[]{:S(2)}, u32[]{:S(2)}) collective-permute-start(f32[48,1152]{1,0:T(8,128)S(1)} %get-tuple-element.47), channel_id=1, source_target_pairs={{0,5},{1,6},{2,7},{3,8},{4,9},{5,10},{6,11},{7,12},{8,13},{9,14},{... | collective-permute-start | bytes 663560
  2070.7 81.6 %collective-permute-start.7 = (f32[36,3456]{1,0:T(8,128)S(1)}, f32[36,3456]{1,0:T(8,128)S(1)}, u32[]{:S(2)}, u32[]{:S(2)}) collective-permute-start(f32[36,3456]{1,0:T(8,128)S(1)} %slice.15), channel_id=1, source_target_pairs={{0,8},{1,9},{2,10},{3,11},{4,12},{5,13},{6,14},{7,15},{8,16},{9,17... | collective-permute-start | bytes 1493000
  2116.5 6.1 collective-permute-start.11
  2121.2 5.8 collective-permute-start.10
  2122.6 10.8 collective-permute-start.9
  2127.0 18.2 collective-permute-start.8
  2133.3 68.7 %copy-start.56 = (f32[1152]{0:T(1024)S(1)}, f32[1152]{0:T(1024)}, u32[]{:S(2)}) copy-start(f32[1152]{0:T(1024)} %get-tuple-element.59) | copy-start | bytes 13828
  2133.3 68.7 %copy-start.57 = (f32[1152]{0:T(1024)S(1)}, f32[1152]{0:T(1024)}, u32[]{:S(2)}) copy-start(f32[1152]{0:T(1024)} %reduce_sum.220) | copy-start | bytes 13828
  2133.3 68.7 %copy-start.66 = (f32[4608]{0:T(1024)S(1)}, f32[4608]{0:T(1024)}, u32[]{:S(2)}) copy-start(f32[4608]{0:T(1024)} %get-tuple-element.69) | copy-start | bytes 55300
  2133.3 68.7 %copy-start.76 = (f32[1152]{0:T(1024)S(1)}, f32[1152]{0:T(1024)}, u32[]{:S(2)}) copy-start(f32[1152]{0:T(1024)} %get-tuple-element.18) | copy-start | bytes 13828
  2133.4 55.9 %collective-permute-start.4 = (f32[48,3456]{1,0:T(8,128)S(1)}, f32[48,3456]{1,0:T(8,128)}, u32[]{:S(2)}, u32[]{:S(2)}) collective-permute-start(f32[48,3456]{1,0:T(8,128)S(1)} %get-tuple-element.46), channel_id=1, source_target_pairs={{0,5},{1,6},{2,7},{3,8},{4,9},{5,10},{6,11},{7,12},{8,13},{9,14},{... | collective-permute-start | bytes 1990664
  2145.3 49.3 %collective-permute-start.3 = (f32[48,3456]{1,0:T(8,128)S(1)}, f32[48,3456]{1,0:T(8,128)}, u32[]{:S(2)}, u32[]{:S(2)}) collective-permute-start(f32[48,3456]{1,0:T(8,128)S(1)} %get-tuple-element.46), channel_id=1, source_target_pairs={{0,4},{1,5},{2,6},{3,7},{4,8},{5,9},{6,10},{7,11},{8,12},{9,13},{1... | collective-permute-start | bytes 1990664
  2152.3 43.9 %collective-permute-start.2 = (f32[48,3456]{1,0:T(8,128)S(1)}, f32[48,3456]{1,0:T(8,128)}, u32[]{:S(2)}, u32[]{:S(2)}) collective-permute-start(f32[48,3456]{1,0:T(8,128)S(1)} %get-tuple-element.46), channel_id=1, source_target_pairs={{0,3},{1,4},{2,5},{3,6},{4,7},{5,8},{6,9},{7,10},{8,11},{9,12},{10... | collective-permute-start | bytes 1990664
  2161.7 166.3 %collective-permute-start.1 = (f32[48,3456]{1,0:T(8,128)S(1)}, f32[48,3456]{1,0:T(8,128)}, u32[]{:S(2)}, u32[]{:S(2)}) collective-permute-start(f32[48,3456]{1,0:T(8,128)S(1)} %get-tuple-element.46), channel_id=1, source_target_pairs={{0,2},{1,3},{2,4},{3,5},{4,6},{5,7},{6,8},{7,9},{8,10},{9,11},{10,... | collective-permute-start | bytes 1990664
  2163.8 165.5 %collective-permute-start = (f32[48,3456]{1,0:T(8,128)S(1)}, f32[48,3456]{1,0:T(8,128)}, u32[]{:S(2)}, u32[]{:S(2)}) collective-permute-start(f32[48,3456]{1,0:T(8,128)S(1)} %get-tuple-element.46), channel_id=1, source_target_pairs={{0,1},{1,2},{2,3},{3,4},{4,5},{5,6},{6,7},{7,8},{8,9},{9,10},{10,1... | collective-permute-start | bytes 1990664
  2189.3 178.7 %collective-permute-start.18 = (f32[40,4608]{1,0:T(8,128)}, f32[40,4608]{1,0:T(8,128)S(1)}, u32[]{:S(2)}, u32[]{:S(2)}) collective-permute-start(f32[40,4608]{1,0:T(8,128)} %get-tuple-element.48), channel_id=1, source_target_pairs={{0,3},{1,4},{2,5},{3,6},{4,7},{5,8},{6,9},{7,10},{8,11},{9,12},{10... | collective-permute-start | bytes 2211848
  2194.5 173.5 %collective-permute-start.17 = (f32[40,4608]{1,0:T(8,128)}, f32[40,4608]{1,0:T(8,128)S(1)}, u32[]{:S(2)}, u32[]{:S(2)}) collective-permute-start(f32[40,4608]{1,0:T(8,128)} %get-tuple-element.48), channel_id=1, source_target_pairs={{0,2},{1,3},{2,4},{3,5},{4,6},{5,7},{6,8},{7,9},{8,10},{9,11},{10,... | collective-permute-start | bytes 2211848
  2196.2 173.5 %collective-permute-start.16 = (f32[40,4608]{1,0:T(8,128)}, f32[40,4608]{1,0:T(8,128)}, u32[]{:S(2)}, u32[]{:S(2)}) collective-permute-start(f32[40,4608]{1,0:T(8,128)} %get-tuple-element.48), channel_id=1, source_target_pairs={{0,1},{1,2},{2,3},{3,4},{4,5},{5,6},{6,7},{7,8},{8,9},{9,10},{10,1... | collective-permute-start | bytes 2211848
  2328.0 40.0 %collective-permute-start.19 = (f32[4,4608]{1,0:T(4,128)S(1)}, f32[4,4608]{1,0:T(4,128)S(1)}, u32[]{:S(2)}, u32[]{:S(2)}) collective-permute-start(f32[4,4608]{1,0:T(4,128)S(1)} %slice.17), channel_id=1, source_target_pairs={{0,4},{1,5},{2,6},{3,7},{4,8},{5,9},{6,10},{7,11},{8,12},{9,13},{1... | collective-permute-start | bytes 221192
  (69 other events, 666.0 us)
Sparse Core Ops, SparseCore 0:
  11.5 82.1 all-gather.19
  97.0 117.8 all-gather.17
  218.4 57.0 all-gather.21
  278.6 90.9 all-gather.23
  371.7 48.8 all-gather.13
  422.5 49.2 all-gather.11
  475.2 86.1 all-gather.15
  606.6 83.7 reduce-scatter.12
  692.7 85.7 reduce-scatter.10
  811.2 76.3 reduce-scatter.14
  894.6 324.8 reduce-scatter.16
where the time goes:
time: 2400 us; the launch traced here: 2390 us
  blocking collectives  1390 us (58%)
  waiting for transfers between devices  541 us (23%)
  matrix products  155 us (6%)
  local copies, waits for them, and re-layouts  151 us (6%)
  starting transfers between devices  109 us (5%)
  other arithmetic  27.4 us (1%)
    unnamed x4, blocking collectives  1370 us
    unnamed x211, local copies, waits for them, and re-layouts  137 us
    all_gather x1, waiting for transfers between devices, per_device(): lax.all_gather(first_local[0], ('lat', 'blk'), axis=0, tiled=True)  109 us
    unnamed x20, starting transfers between devices  108 us
    all_gather x1, waiting for transfers between devices, per_device(): lax.all_gather(second_local[0], ('lat', 'blk'), axis=0, tiled=True)  89.1 us
    reduce_scatter x1, waiting for transfers between devices, per_device(): lax.psum_scatter(grad_keys, 'blk', scatter_dimension=1, tiled=True)  85.6 us
    all_gather x1, waiting for transfers between devices, per_device(): lax.all_gather(second_local[2], ('lat', 'blk'), axis=0, tiled=True)  58.5 us
    reduce_scatter x1, waiting for transfers between devices, per_device(): lax.psum_scatter(grad_values, 'blk', scatter_dimension=1, tiled=True)  54.7 us
  transfers between devices with their start and end apart: 31, of which 9 were waited for; matrix products, arithmetic and copies ran while one was open for 61% of the time, Pallas kernels for 0%

commit v1 on v0

v1 whole, which is shorter than its diff:
```python
import math

import jax
import jax.numpy as jnp
from jax import lax
from jax.experimental import pallas as pl
from jax.experimental.pallas import tpu as pltpu
from jax.sharding import PartitionSpec as P

H = 16
EPS = 1e-06
GELU_C = 0.7978845608028654
CUBIC = 0.044715
HIGH = lax.Precision.HIGHEST
BOTH = ("lat", "blk")
F32 = jnp.float32
BF16 = jnp.bfloat16


def layer_norm(value):
    mean = jnp.mean(value, axis=-1, keepdims=True)
    centered = value - mean
    rstd = lax.rsqrt(jnp.mean(centered * centered, axis=-1, keepdims=True) + EPS)
    return (centered * rstd, rstd)


def norm_back(grad, normed, rstd):
    return (
        grad
        - jnp.mean(grad, axis=-1, keepdims=True)
        - normed * jnp.mean(grad * normed, axis=-1, keepdims=True)
    ) * rstd


def silu_slope(value):
    sigma = jax.nn.sigmoid(value)
    return sigma * (1.0 + value * (1.0 - sigma))


def dot(left, right):
    return jnp.dot(left, right, preferred_element_type=F32)


def dot_nt(left, right):
    return lax.dot_general(left, right, (((1,), (1,)), ((), ())), preferred_element_type=F32)


def dot_tn(left, right):
    return lax.dot_general(left, right, (((0,), (0,)), ((), ())), preferred_element_type=F32)


def scatter_rows(term, n):
    pieces = term.astype(BF16).reshape(n, term.shape[0] // n, term.shape[1])
    return lax.psum_scatter(pieces, BOTH, scatter_dimension=0).astype(F32)


MESH = pl.DeviceIdType.MESH
VMEM = pltpu.VMEM


def flip(index, bit):
    return index + bit - 2 * bit * ((index // bit) % 2)


def place(bias_ref, start, total):
    count = bias_ref.shape[1]
    row = lax.broadcasted_iota(jnp.int32, (count, total), 0)
    col = lax.broadcasted_iota(jnp.int32, (count, total), 1)
    spot = jnp.where(col == row + start, 1.0, 0.0).astype(BF16)
    return dot(bias_ref[...].astype(BF16), spot)


class Spread:
    def __init__(self, full, own, rows, halves, sems, l, z):
        self.full, self.own, self.rows, self.halves = full, own, rows, halves
        self.send, self.recv = sems
        self.l, self.z = l, z
        self.lx, self.ly, self.lc = flip(l, 2), flip(l, 4), flip(l, 1)
        self.lxy = flip(self.lx, 4)

    def view(self, lat, half=None):
        start = pl.multiple_of(lat * self.rows, 16)
        if half is None:
            return self.full.at[pl.ds(start, self.rows), :]
        (row, row_count), (col, col_count) = self.halves[half]
        return self.full.at[pl.ds(pl.multiple_of(start + row, 16), row_count), pl.ds(col, col_count)]

    def copy(self, k, src, dst, to):
        return pltpu.make_async_remote_copy(
            src_ref=src,
            dst_ref=dst,
            send_sem=self.send.at[k],
            recv_sem=self.recv.at[k],
            device_id=(to, self.z),
            device_id_type=MESH,
        )

    def out(self, k):
        l, lx, ly, lc, lxy = self.l, self.lx, self.ly, self.lc, self.lxy
        own = self.own
        return [
            lambda: self.copy(0, own, self.view(l), lx),
            lambda: self.copy(1, own, self.view(l), ly),
            lambda: self.copy(2, self.view(lx, 0), self.view(lx, 0), ly),
            lambda: self.copy(3, self.view(ly, 1), self.view(ly, 1), lx),
            lambda: self.copy(4, own, self.view(l), lc),
            lambda: self.copy(5, self.view(lx), self.view(lx), lc),
            lambda: self.copy(6, self.view(ly), self.view(ly), lc),
            lambda: self.copy(7, self.view(lxy, 0), self.view(lxy, 0), lc),
            lambda: self.copy(8, self.view(lxy, 1), self.view(lxy, 1), lc),
        ][k]()

    def arrival(self, k):
        lx, ly, lc, lxy = self.lx, self.ly, self.lc, self.lxy
        lat, half, sender = [
            (lx, None, lx),
            (ly, None, ly),
            (lxy, 0, ly),
            (lxy, 1, lx),
            (lc, None, lc),
            (flip(lc, 2), None, lc),
            (flip(lc, 4), None, lc),
            (flip(flip(lc, 2), 4), 0, lc),
            (flip(flip(lc, 2), 4), 1, lc),
        ][k]
        here = self.view(lat, half)
        return self.copy(k, here, here, sender)

    def start(self):
        for k in (0, 1, 4):
            self.out(k).start()

    def pass_x(self):
        self.arrival(0).wait_recv()
        self.out(2).start()
        self.out(5).start()

    def pass_y(self):
        self.arrival(1).wait_recv()
        self.out(3).start()
        self.out(6).start()

    def pass_core(self):
        self.arrival(2).wait_recv()
        self.out(7).start()
        self.arrival(3).wait_recv()
        self.out(8).start()

    def finish(self):
        for k in range(4, 9):
            self.arrival(k).wait_recv()

    def drain(self):
        for k in range(9):
            self.out(k).wait_send()


def forward_kernel(
    cond_ref, tokens_ref, ada_ref, qkv_ref, proj_ref, up_ref, down_ref,
    ada_b, q_b, v_b, p_b, d_b, u_b,
    vec_out, cond_out, up_full, down_full, proj_full, qkv_full, in_all, q_out, k_out, v_out, mixed_out, lse_out, attn_out,
    act_s, part, part_in, mod_z, normed_s, wide_s, qkv_s, qkv_z, proj_s, proj_z, up_s, up_z, up_own, proj_own, down_s, turned, joined,
    sem_a, sem_b, sem_c, sem_z, sem_in, sem_at, sem_send, sem_recv, sem_l,
):
    l, z = lax.axis_index("lat"), lax.axis_index("blk")
    nl, nb = cond_out.shape[0], in_all.shape[0]
    index = l * nb + z
    width = tokens_ref.shape[1]
    rows = tokens_ref.shape[0]
    share = proj_ref.shape[0]
    local = width // nb
    size = width // H
    heads = H // nb
    hidden_size = up_ref.shape[1]
    column = nb * share
    scale = 1.0 / math.sqrt(size)

    def lat_at(distance):
        at = l
        for bit in (1, 2, 4):
            if distance & bit:
                at = flip(at, bit)
        return at

    def blk_at(step):
        return lax.rem(z + step, nb)

    def remote(src, dst, send, recv, lat, blk):
        return pltpu.make_async_remote_copy(
            src_ref=src, dst_ref=dst, send_sem=send, recv_sem=recv, device_id=(lat, blk), device_id_type=MESH
        )

    barrier = pltpu.get_barrier_semaphore()
    for d in range(1, nl):
        pl.semaphore_signal(barrier, inc=1, device_id=(lat_at(d), z), device_id_type=MESH)
    for j in range(1, nb):
        pl.semaphore_signal(barrier, inc=1, device_id=(l, blk_at(j)), device_id_type=MESH)
    pl.semaphore_wait(barrier, nl + nb - 2)

    cond = cond_ref[...]
    cond_act = cond / (1.0 + jnp.exp(-cond))
    act_s[...] = cond_act
    cond_out[l] = cond_act
    cond_copies = [
        remote(act_s, cond_out.at[l], sem_a.at[0, d], sem_a.at[1, d], lat_at(d), z) for d in range(1, nl)
    ]
    for copy in cond_copies:
        copy.start()

    for b in range(nb):
        for third in range(3):
            at = third * width + b * local
            qkv_s[b, 0:share, third * local : (third + 1) * local] = qkv_ref[:, at : at + local].astype(BF16)
    proj_s[0:share, :] = proj_ref[...].astype(BF16)
    down_s[...] = down_ref[...].astype(BF16)
    for c in range(hidden_size // width):
        wide_s[c * share : (c + 1) * share, 0:width] = up_ref[:, c * width : (c + 1) * width]
    up_s[...] = wide_s[:, 0:width].astype(BF16)

    def blk_copies(k, src_of, dst_of):
        out, come = [], []
        for j in range(1, nb):
            to, sender = blk_at(j), blk_at(nb - j)
            out.append(remote(src_of(to), dst_of(z), sem_z.at[0, k, j], sem_z.at[1, k, j], l, to))
            come.append(remote(src_of(to), dst_of(sender), sem_z.at[0, k, j], sem_z.at[1, k, j], l, sender))
        return out, come

    down_start = l * (nb * down_s.shape[0])

    def down_slot(b):
        start = pl.multiple_of(down_start + b * down_s.shape[0], 16)
        return down_full.at[pl.ds(start, down_s.shape[0]), :]

    qkv_out_z, qkv_in_z = blk_copies(0, lambda to: qkv_s.at[to], lambda b: qkv_z.at[b])
    proj_out_z, proj_in_z = blk_copies(1, lambda to: proj_s, lambda b: proj_z.at[b])
    up_out_z, up_in_z = blk_copies(2, lambda to: up_s, lambda b: up_z.at[b])
    down_out_z, down_in_z = blk_copies(3, lambda to: down_s, down_slot)
    for copy in qkv_out_z + proj_out_z + up_out_z:
        copy.start()
    own_down = pltpu.make_async_copy(down_s, down_slot(z), sem_l.at[0])
    own_down.start()
    qkv_z[z] = qkv_s[z]
    proj_z[z] = proj_s[...]
    up_z[z] = up_s[...]

    offsets = jnp.concatenate(
        [place(ada_b, index * ada_b.shape[1], 6 * width)]
        + [place(b, index * share, width) for b in (q_b, v_b, p_b, d_b)]
        + [place(u_b, index * u_b.shape[1], hidden_size)],
        axis=1,
    )

    lanes = lax.broadcasted_iota(jnp.int32, (nl, width), 0)
    for d in range(1, nl):
        remote(act_s, cond_out.at[lat_at(d)], sem_a.at[0, d], sem_a.at[1, d], lat_at(d), z).wait_recv()
    every = jnp.zeros((nl, width), F32)
    for i in range(nl):
        every = jnp.where(lanes == i, jnp.broadcast_to(cond_out[i], (nl, width)), every)
    row = lax.broadcasted_iota(jnp.int32, (width, share), 0)
    col = lax.broadcasted_iota(jnp.int32, (width, share), 1)
    pick = jnp.where(row == col + index * share, 1.0, 0.0).astype(BF16)
    picked = dot(every.astype(BF16), pick).astype(BF16)
    product = dot(picked, ada_ref[...].astype(BF16))
    for i in range(nl):
        part[i, :, 0 : 6 * width] = product[i : i + 1, :] + offsets[:, 0 : 6 * width]
        part[i, :, 6 * width :] = offsets[:, 6 * width :]
    part_copies = []
    for d in range(1, nl):
        to = lat_at(d)
        part_copies.append(remote(part.at[to], part_in.at[l], sem_b.at[0, d], sem_b.at[1, d], to, z))
        part_copies[-1].start()
    part_in[l] = part[l]

    value = tokens_ref[...]
    centered = value - jnp.mean(value, axis=-1, keepdims=True)
    normed_s[...] = centered * lax.rsqrt(jnp.mean(centered * centered, axis=-1, keepdims=True) + EPS)

    for d in range(1, nl):
        remote(part.at[l], part_in.at[lat_at(d)], sem_b.at[0, d], sem_b.at[1, d], lat_at(d), z).wait_recv()
    total = part_in[0]
    for i in range(1, nl):
        total = total + part_in[i]
    mod_z[z] = total
    mod_copies = []
    for j in range(1, nb):
        mod_copies.append(remote(mod_z.at[z], mod_z.at[z], sem_c.at[0, j], sem_c.at[1, j], l, blk_at(j)))
        mod_copies[-1].start()

    def gather_column(slots, wide, dst, at):
        for b in range(nb):
            wide_s[b * share : (b + 1) * share, 0:wide] = slots[b].astype(F32)[0:share, :]
        dst[at, :] = wide_s[:, 0:wide].astype(BF16)

    whole = slice(None)
    mine = pl.ds(pl.multiple_of(l * column, 16), column)

    def sems(w):
        return sem_send.at[w], sem_recv.at[w]

    low = column // 32 * 16 + 16 if column % 32 else column // 2
    rows_low = (((0, low), (0, width)), ((low, column - low), (0, width)))
    rows_high = (((0, column - low), (0, 3 * local)), ((column - low, low), (0, 3 * local)))
    half = hidden_size // 2
    tall = nb * down_s.shape[0]
    spread_qkv = Spread(qkv_full, qkv_full.at[mine, :], column, rows_high, sems(0), l, z)
    spread_proj = Spread(proj_full, proj_own, column, rows_low, sems(1), l, z)
    spread_up = Spread(up_full, up_own, column, (((0, column), (0, half)), ((0, column), (half, half))), sems(2), l, z)
    spread_down = Spread(
        down_full,
        down_full.at[pl.ds(pl.multiple_of(down_start, 16), tall), :],
        tall,
        (((0, tall // 2), (0, width)), ((tall // 2, tall // 2), (0, width))),
        sems(3),
        l,
        z,
    )

    for copy in qkv_in_z:
        copy.wait_recv()
    gather_column(qkv_z, 3 * local, qkv_full, mine)
    spread_qkv.start()
    for copy in proj_in_z:
        copy.wait_recv()
    gather_column(proj_z, width, proj_own, whole)
    spread_proj.start()
    own_proj = pltpu.make_async_copy(proj_own, proj_full.at[mine, :], sem_l.at[1])
    own_proj.start()

    for j in range(1, nb):
        sender = blk_at(nb - j)
        remote(mod_z.at[sender], mod_z.at[sender], sem_c.at[0, j], sem_c.at[1, j], l, sender).wait_recv()
    vec = mod_z[0]
    for b in range(1, nb):
        vec = vec + mod_z[b]
    vec_out[...] = vec
    in_all[z] = (normed_s[...] * (1.0 + vec[:, width : 2 * width]) + vec[:, 0:width]).astype(BF16)
    in_out, in_in = [], []
    for j in range(1, nb):
        to, sender = blk_at(j), blk_at(nb - j)
        in_out.append(remote(in_all.at[z], in_all.at[z], sem_in.at[0, j], sem_in.at[1, j], l, to))
        in_in.append(remote(in_all.at[sender], in_all.at[sender], sem_in.at[0, j], sem_in.at[1, j], l, sender))
        in_out[-1].start()
    for copy in down_out_z:
        copy.start()

    for copy in up_in_z:
        copy.wait_recv()
    for c in range(hidden_size // width):
        for b in range(nb):
            wide_s[b * share : (b + 1) * share, 0:width] = up_z[b].astype(F32)[c * share : (c + 1) * share, :]
        up_own[:, c * width : (c + 1) * width] = wide_s[:, 0:width].astype(BF16)
    spread_up.start()
    own_up = pltpu.make_async_copy(up_own, up_full.at[mine, :], sem_l.at[2])
    own_up.start()

    spread_qkv.pass_x()
    spread_qkv.pass_y()
    spread_qkv.pass_core()
    spread_qkv.finish()

    q_off = jnp.zeros((1, local), F32)
    v_off = jnp.zeros((1, local), F32)
    for b in range(nb):
        at = 6 * width + b * local
        q_off = jnp.where(z == b, vec[:, at : at + local], q_off)
        v_off = jnp.where(z == b, vec[:, at + width : at + width + local], v_off)
    shift = jnp.concatenate([q_off, jnp.zeros((1, local), F32), v_off], axis=1)

    def project(b):
        block = dot(in_all[b], qkv_full[...]) + shift
        for h in range(heads):
            at = h * size
            q_out[h, b] = block[:, at : at + size].astype(BF16)
            k_out[h, b] = block[:, local + at : local + at + size].astype(BF16)
            value = block[:, 2 * local + at : 2 * local + at + size]
            v_out[h, b] = value.astype(BF16)
            turned[h, b] = value.T.astype(BF16)

    project(z)
    spread_proj.pass_x()
    spread_proj.pass_y()
    for j in range(1, nb):
        in_in[j - 1].wait_recv()
        project(blk_at(nb - j))
    spread_up.pass_x()
    spread_up.pass_y()
    own_down.wait()
    for copy in down_in_z:
        copy.wait_recv()
    spread_down.start()

    factor = scale * 1.4426950408889634

    def attend(step, carry):
        j, h = step // heads, lax.rem(step, heads)
        b = lax.rem(z + 1 + j, nb)
        keys = k_out[h].reshape(nb * rows, size)
        raw = dot_nt(keys, q_out[h, b])
        top = jnp.max(raw, axis=0, keepdims=True)
        expo = jnp.exp2(raw * factor - top * factor)
        norm = jnp.sum(expo, axis=0, keepdims=True)
        lse_out[h, b] = top * scale + jnp.log(norm)
        expo16 = expo.astype(BF16)
        mixed = dot(turned[h, 0], expo16[0:rows])
        for other in range(1, nb):
            mixed = mixed + dot(turned[h, other], expo16[other * rows : (other + 1) * rows])
        mixed_out[h, b] = (mixed / norm).T.astype(BF16)
        return carry

    lax.fori_loop(0, nb * heads, attend, 0)
    for j in range(nb):
        b = lax.rem(z + 1 + j, nb)
        for h in range(heads):
            joined[b, :, h * size : (h + 1) * size] = mixed_out[h, b]
        if j < nb - 1:
            remote(joined.at[b], attn_out.at[z], sem_at.at[0, j], sem_at.at[1, j], l, b).start()
    attn_out[z] = joined[z]

    spread_proj.pass_core()
    spread_up.pass_core()
    spread_down.pass_x()
    spread_down.pass_y()
    spread_down.pass_core()
    own_up.wait()
    own_proj.wait()
    for j in range(nb - 1):
        sender = blk_at(nb - 1 - j)
        remote(joined.at[z], attn_out.at[sender], sem_at.at[0, j], sem_at.at[1, j], l, sender).wait_recv()
    for spread in (spread_proj, spread_up, spread_down):
        spread.finish()
    for spread in (spread_qkv, spread_proj, spread_up, spread_down):
        spread.drain()
    for copy in cond_copies + part_copies + mod_copies + in_out:
        copy.wait_send()
    for copy in qkv_out_z + proj_out_z + up_out_z + down_out_z:
        copy.wait_send()
    for j in range(nb - 1):
        to = blk_at(1 + j)
        remote(joined.at[to], attn_out.at[z], sem_at.at[0, j], sem_at.at[1, j], l, to).wait_send()


def forward(nl, nb, tokens, condition, weights, biases):
    ada, qkv, proj, up, down = weights
    rows, width = tokens.shape
    share, hidden_size, down_rows = proj.shape[0], up.shape[1], down.shape[0]
    local, heads, column, size = width // nb, H // nb, nb * share, width // H
    pad = -(-share // 16) * 16
    total = 6 * width + 4 * width + hidden_size
    sd = jax.ShapeDtypeStruct
    in_vmem, in_hbm = pl.BlockSpec(memory_space=VMEM), pl.BlockSpec(memory_space=pl.ANY)
    outs = [
        (sd((1, total), F32), in_vmem),
        (sd((nl, 1, width), F32), in_vmem),
        (sd((width, hidden_size), BF16), in_hbm),
        (sd((hidden_size, width), BF16), in_hbm),
        (sd((width, width), BF16), in_hbm),
        (sd((width, 3 * local), BF16), in_vmem),
        (sd((nb, rows, width), BF16), in_vmem),
        (sd((heads, nb, rows, size), BF16), in_vmem),
        (sd((heads, nb, rows, size), BF16), in_vmem),
        (sd((heads, nb, rows, size), BF16), in_vmem),
        (sd((heads, nb, rows, size), BF16), in_vmem),
        (sd((heads, nb, 1, rows), F32), in_vmem),
        (sd((nb, rows, local), BF16), in_vmem),
    ]
    dma = pltpu.SemaphoreType.DMA
    scratch = [
        VMEM((1, width), F32),
        VMEM((nl, 1, total), F32),
        VMEM((nl, 1, total), F32),
        VMEM((nb, 1, total), F32),
        VMEM((rows, width), F32),
        VMEM((column, width), F32),
        VMEM((nb, pad, 3 * local), BF16),
        VMEM((nb, pad, 3 * local), BF16),
        VMEM((pad, width), BF16),
        VMEM((nb, pad, width), BF16),
        VMEM((share * hidden_size // width, width), BF16),
        VMEM((nb, share * hidden_size // width, width), BF16),
        VMEM((column, hidden_size), BF16),
        VMEM((column, width), BF16),
        VMEM((down_rows, width), BF16),
        VMEM((heads, nb, size, rows), BF16),
        VMEM((nb, rows, local), BF16),
        dma((2, nl)),
        dma((2, nl)),
        dma((2, nb)),
        dma((2, 4, nb)),
        dma((2, nb)),
        dma((2, nb)),
        dma((4, 9)),
        dma((4, 9)),
        dma((3,)),
    ]
    args = [condition, tokens, ada, qkv, proj, up, down] + [bias.reshape(1, -1) for bias in biases]
    return pl.pallas_call(
        forward_kernel,
        out_shape=[shape for shape, _ in outs],
        in_specs=[in_vmem] * len(args),
        out_specs=[spec for _, spec in outs],
        scratch_shapes=scratch,
        compiler_params=pltpu.CompilerParams(
            collective_id=0, has_side_effects=True, vmem_limit_bytes=56 * 2**20
        ),
        name="forward",
    )(*args)


def fused(
    tokens,
    condition,
    cotangent,
    ada_weight,
    ada_bias,
    qkv_weight,
    query_bias,
    value_bias,
    proj_weight,
    proj_bias,
    up_weight,
    up_bias,
    down_weight,
    down_bias,
):
    tokens, cotangent = tokens[0], cotangent[0]
    rows, width = tokens.shape
    nb, nl = lax.axis_size("blk"), lax.axis_size("lat")
    n = nb * nl
    my_lat, my_blk = lax.axis_index("lat"), lax.axis_index("blk")
    index = my_lat * nb + my_blk
    hidden_size = up_weight.shape[1]
    share = width // n
    heads = H // nb
    size = width // H
    local = heads * size
    seq = rows * nb
    scale = 1.0 / math.sqrt(size)

    weights = (ada_weight, qkv_weight, proj_weight, up_weight, down_weight)
    biases = (ada_bias, query_bias, value_bias, proj_bias, down_bias, up_bias)
    vec, cond_all, up_matrix, down_matrix, out_matrix, qkv_cols, in_all, query, keys, values, mixed, lse, attn = forward(
        nl, nb, tokens, condition, weights, biases
    )
    shift1, scale1, gate1, shift2, scale2, gate2 = [vec[:, i * width : (i + 1) * width] for i in range(6)]
    out_off, down_off = [vec[:, i * width : (i + 1) * width] for i in (8, 9)]
    up_off = vec[:, 10 * width :]
    picked = lax.dynamic_slice_in_dim(cond_all[:, 0], index * share, share, axis=1)
    ada16 = ada_weight.astype(BF16)
    normed1, rstd1 = layer_norm(tokens)
    attn_in_all = in_all.reshape(seq, width)
    query, keys, values, mixed = [a.reshape(heads, seq, size) for a in (query, keys, values, mixed)]
    log_total = lse.reshape(heads, seq, 1)
    attn = attn.transpose(1, 0, 2).reshape(rows, width)

    proj = dot(attn, out_matrix) + out_off
    mid = tokens + gate1 * proj
    normed2, rstd2 = layer_norm(mid)
    mlp_in = (normed2 * (1.0 + scale2) + shift2).astype(BF16)
    hidden = dot(mlp_in, up_matrix) + up_off
    inner = jnp.tanh(GELU_C * (hidden + CUBIC * hidden * hidden * hidden))
    act = (0.5 * hidden * (1.0 + inner)).astype(BF16)
    slope = 0.5 * (1.0 + inner) + 0.5 * hidden * (1.0 - inner * inner) * GELU_C * (
        1.0 + 3.0 * CUBIC * hidden * hidden
    )
    mlp_out = dot(act, down_matrix) + down_off
    output = mid + gate2 * mlp_out

    grad_gate2 = jnp.sum(cotangent * mlp_out, axis=0, keepdims=True)
    d_mlp = cotangent * gate2
    d_mlp16 = d_mlp.astype(BF16)
    down_term = dot_tn(act, d_mlp16)
    d_hidden = dot_nt(d_mlp16, down_matrix) * slope
    d_hidden16 = d_hidden.astype(BF16)
    up_term = dot_tn(mlp_in, d_hidden16)
    down_grad = scatter_rows(down_term, n)
    up_grad = scatter_rows(up_term, n)
    d_mlp_in = dot_nt(d_hidden16, up_matrix)
    grad_shift2 = jnp.sum(d_mlp_in, axis=0, keepdims=True)
    grad_scale2 = jnp.sum(d_mlp_in * normed2, axis=0, keepdims=True)
    d_mid = cotangent + norm_back(d_mlp_in * (1.0 + scale2), normed2, rstd2)
    grad_gate1 = jnp.sum(d_mid * proj, axis=0, keepdims=True)
    d_proj = d_mid * gate1
    d_proj16 = d_proj.astype(BF16)
    proj_grad = scatter_rows(dot_tn(attn, d_proj16), n)
    d_attn = dot_nt(d_proj16, out_matrix).astype(BF16)

    d_attn = d_attn.reshape(rows, nb, heads, size).transpose(1, 2, 0, 3)
    d_attn = lax.all_to_all(d_attn, "blk", 0, 0).transpose(1, 0, 2, 3).reshape(heads, seq, size)
    delta = jnp.sum(d_attn.astype(F32) * mixed.astype(F32), axis=-1, keepdims=True)
    scores = jnp.einsum("hqd,hkd->hqk", query, keys, preferred_element_type=F32) * scale
    probs = jnp.exp(scores - log_total)
    d_values = jnp.einsum("hqk,hqd->hkd", probs.astype(BF16), d_attn, preferred_element_type=F32)
    d_probs = jnp.einsum("hqd,hkd->hqk", d_attn, values, preferred_element_type=F32)
    d_scores = (probs * (d_probs - delta) * scale).astype(BF16)
    d_query = jnp.einsum("hqk,hkd->hqd", d_scores, keys, preferred_element_type=F32)
    d_keys = jnp.einsum("hqk,hqd->hkd", d_scores, query, preferred_element_type=F32)
    query_bias_term = jnp.sum(d_query, axis=1).reshape(local)
    value_bias_term = jnp.sum(d_values, axis=1).reshape(local)
    d_qkv = jnp.stack([d_query, d_keys, d_values]).astype(BF16)
    d_qkv = d_qkv.transpose(2, 0, 1, 3).reshape(seq, 3 * local)
    d_attn_in = dot_nt(d_qkv, qkv_cols)
    d_attn_in = lax.psum_scatter(
        d_attn_in.astype(BF16).reshape(nb, rows, width), "blk", scatter_dimension=0
    ).astype(F32)
    qkv_term = dot_tn(attn_in_all, d_qkv).astype(BF16).reshape(nl, nb * share, 3 * local)
    qkv_part = lax.psum_scatter(qkv_term, "lat", scatter_dimension=0)
    qkv_part = lax.all_to_all(qkv_part.reshape(nb, share, 3 * local), "blk", 0, 0)
    qkv_grad = qkv_part.reshape(nb, share, 3, local).transpose(1, 2, 0, 3).reshape(share, 3 * width)
    qkv_grad = qkv_grad.astype(F32)

    grad_shift1 = jnp.sum(d_attn_in, axis=0, keepdims=True)
    grad_scale1 = jnp.sum(d_attn_in * normed1, axis=0, keepdims=True)
    grad_tokens = d_mid + norm_back(d_attn_in * (1.0 + scale1), normed1, rstd1)

    zero = jnp.zeros((width,), F32)
    bias_terms = [
        lax.dynamic_update_slice(zero, query_bias_term, (my_blk * local,)),
        lax.dynamic_update_slice(zero, value_bias_term, (my_blk * local,)),
        jnp.sum(d_proj, axis=0),
        jnp.sum(d_mlp, axis=0),
        jnp.sum(d_hidden, axis=0),
    ]
    bias_term = jnp.concatenate([term.reshape(n, -1) for term in bias_terms], axis=1)
    bias_grad = lax.psum_scatter(bias_term, BOTH, scatter_dimension=0)
    cuts = [share, 2 * share, 3 * share, 4 * share]
    q_grad, v_grad, out_grad, db_grad, ub_grad = jnp.split(bias_grad, cuts)

    d_mod = jnp.concatenate(
        [grad_shift1, grad_scale1, grad_gate1, grad_shift2, grad_scale2, grad_gate2], axis=1
    )
    d_mod = lax.all_gather(lax.psum(d_mod, "blk"), "lat", axis=0, tiled=True)
    ada_grad = lax.dot_general(picked, d_mod, (((0,), (0,)), ((), ())), precision=HIGH)
    mod_total = jnp.sum(d_mod, axis=0)
    ada_bias_grad = lax.dynamic_slice(mod_total, (index * ada_bias.shape[0],), ada_bias.shape)
    back_cond = lax.dot_general(
        d_mod, ada16.astype(F32), (((1,), (1,)), ((), ())), precision=HIGH
    )
    back_cond = lax.all_gather(back_cond, BOTH, axis=0)
    back_cond = lax.dynamic_index_in_dim(back_cond, my_lat, axis=1, keepdims=False)
    grad_condition = back_cond.reshape(1, width) * silu_slope(condition)
    return (
        output[None],
        grad_tokens[None],
        grad_condition,
        ada_grad,
        ada_bias_grad,
        qkv_grad,
        q_grad,
        v_grad,
        proj_grad,
        out_grad,
        up_grad,
        ub_grad,
        down_grad,
        db_grad,
    )


def generic(
    tokens,
    condition,
    cotangent,
    ada_weight,
    ada_bias,
    qkv_weight,
    query_bias,
    value_bias,
    proj_weight,
    proj_bias,
    up_weight,
    up_bias,
    down_weight,
    down_bias,
):
    tokens, cotangent = tokens[0], cotangent[0]
    rows, width = tokens.shape
    nb, nl = lax.axis_size("blk"), lax.axis_size("lat")
    n = nb * nl
    my_lat, my_blk = lax.axis_index("lat"), lax.axis_index("blk")
    index = my_lat * nb + my_blk
    hidden_size = up_weight.shape[1]
    share = width // n
    heads = H // nb
    size = width // H
    local = heads * size
    seq = rows * nb
    scale = 1.0 / math.sqrt(size)

    cond_act = jax.nn.silu(condition)
    cond_all = lax.all_gather(cond_act, "lat", axis=0, tiled=True)
    picked = lax.dynamic_slice_in_dim(cond_all, index * share, share, axis=1)
    ada16 = ada_weight.astype(BF16)
    offset = lax.dynamic_update_slice(
        jnp.zeros((6 * width,), F32), ada_bias.astype(BF16).astype(F32), (index * ada_bias.shape[0],)
    )
    mod_part = dot(picked.astype(BF16), ada16) + offset[None, :]
    mod_part = lax.psum(mod_part, BOTH)
    modulation = lax.dynamic_slice_in_dim(mod_part, my_lat, 1, axis=0)
    shift1, scale1, gate1, shift2, scale2, gate2 = jnp.split(modulation, 6, axis=1)

    small = jnp.concatenate([query_bias, value_bias, proj_bias, down_bias, up_bias]).astype(BF16)
    small = lax.all_gather(small, BOTH, axis=0).astype(F32)
    q_off, v_off, out_off, down_off = [
        small[:, i * share : (i + 1) * share].reshape(1, width) for i in range(4)
    ]
    up_off = small[:, 4 * share :].reshape(1, hidden_size)
    q_off = lax.dynamic_slice_in_dim(q_off, my_blk * local, local, axis=1)
    v_off = lax.dynamic_slice_in_dim(v_off, my_blk * local, local, axis=1)

    cut = qkv_weight.astype(BF16).reshape(share, 3, nb, local).transpose(2, 0, 1, 3)
    cut = lax.all_to_all(cut.reshape(nb, share, 3 * local), "blk", 0, 0)
    qkv_cols = lax.all_gather(cut.reshape(nb * share, 3 * local), "lat", axis=0, tiled=True)
    out_matrix = lax.all_gather(proj_weight.astype(BF16), BOTH, axis=0, tiled=True)
    up_matrix = lax.all_gather(up_weight.astype(BF16), BOTH, axis=0, tiled=True)
    down_matrix = lax.all_gather(down_weight.astype(BF16), BOTH, axis=0, tiled=True)

    normed1, rstd1 = layer_norm(tokens)
    attn_in = (normed1 * (1.0 + scale1) + shift1).astype(BF16)
    attn_in_all = lax.all_gather(attn_in, "blk", axis=0, tiled=True)
    offsets = jnp.concatenate([q_off, jnp.zeros_like(q_off), v_off], axis=1)
    qkv = (dot(attn_in_all, qkv_cols) + offsets).astype(BF16)
    qkv = qkv.reshape(seq, 3, heads, size).transpose(1, 2, 0, 3)
    query, keys, values = qkv[0], qkv[1], qkv[2]
    scores = jnp.einsum("hqd,hkd->hqk", query, keys, preferred_element_type=F32) * scale
    peak = jnp.max(scores, axis=-1, keepdims=True)
    expo = jnp.exp(scores - peak)
    total = jnp.sum(expo, axis=-1, keepdims=True)
    accum = jnp.einsum("hqk,hkd->hqd", expo.astype(BF16), values, preferred_element_type=F32)
    log_total = peak + jnp.log(total)
    mixed = (accum / total).astype(BF16)
    back = lax.all_to_all(mixed.reshape(heads, nb, rows, size).transpose(1, 2, 0, 3), "blk", 0, 0)
    attn = back.transpose(1, 0, 2, 3).reshape(rows, width)

    proj = dot(attn, out_matrix) + out_off
    mid = tokens + gate1 * proj
    normed2, rstd2 = layer_norm(mid)
    mlp_in = (normed2 * (1.0 + scale2) + shift2).astype(BF16)
    hidden = dot(mlp_in, up_matrix) + up_off
    inner = jnp.tanh(GELU_C * (hidden + CUBIC * hidden * hidden * hidden))
    act = (0.5 * hidden * (1.0 + inner)).astype(BF16)
    slope = 0.5 * (1.0 + inner) + 0.5 * hidden * (1.0 - inner * inner) * GELU_C * (
        1.0 + 3.0 * CUBIC * hidden * hidden
    )
    mlp_out = dot(act, down_matrix) + down_off
    output = mid + gate2 * mlp_out

    grad_gate2 = jnp.sum(cotangent * mlp_out, axis=0, keepdims=True)
    d_mlp = cotangent * gate2
    d_mlp16 = d_mlp.astype(BF16)
    down_term = dot_tn(act, d_mlp16)
    d_hidden = dot_nt(d_mlp16, down_matrix) * slope
    d_hidden16 = d_hidden.astype(BF16)
    up_term = dot_tn(mlp_in, d_hidden16)
    down_grad = scatter_rows(down_term, n)
    up_grad = scatter_rows(up_term, n)
    d_mlp_in = dot_nt(d_hidden16, up_matrix)
    grad_shift2 = jnp.sum(d_mlp_in, axis=0, keepdims=True)
    grad_scale2 = jnp.sum(d_mlp_in * normed2, axis=0, keepdims=True)
    d_mid = cotangent + norm_back(d_mlp_in * (1.0 + scale2), normed2, rstd2)
    grad_gate1 = jnp.sum(d_mid * proj, axis=0, keepdims=True)
    d_proj = d_mid * gate1
    d_proj16 = d_proj.astype(BF16)
    proj_grad = scatter_rows(dot_tn(attn, d_proj16), n)
    d_attn = dot_nt(d_proj16, out_matrix).astype(BF16)

    d_attn = d_attn.reshape(rows, nb, heads, size).transpose(1, 2, 0, 3)
    d_attn = lax.all_to_all(d_attn, "blk", 0, 0).transpose(1, 0, 2, 3).reshape(heads, seq, size)
    delta = jnp.sum(d_attn.astype(F32) * mixed.astype(F32), axis=-1, keepdims=True)
    scores = jnp.einsum("hqd,hkd->hqk", query, keys, preferred_element_type=F32) * scale
    probs = jnp.exp(scores - log_total)
    d_values = jnp.einsum("hqk,hqd->hkd", probs.astype(BF16), d_attn, preferred_element_type=F32)
    d_probs = jnp.einsum("hqd,hkd->hqk", d_attn, values, preferred_element_type=F32)
    d_scores = (probs * (d_probs - delta) * scale).astype(BF16)
    d_query = jnp.einsum("hqk,hkd->hqd", d_scores, keys, preferred_element_type=F32)
    d_keys = jnp.einsum("hqk,hqd->hkd", d_scores, query, preferred_element_type=F32)
    query_bias_term = jnp.sum(d_query, axis=1).reshape(local)
    value_bias_term = jnp.sum(d_values, axis=1).reshape(local)
    d_qkv = jnp.stack([d_query, d_keys, d_values]).astype(BF16)
    d_qkv = d_qkv.transpose(2, 0, 1, 3).reshape(seq, 3 * local)
    d_attn_in = dot_nt(d_qkv, qkv_cols)
    d_attn_in = lax.psum_scatter(
        d_attn_in.astype(BF16).reshape(nb, rows, width), "blk", scatter_dimension=0
    ).astype(F32)
    qkv_term = dot_tn(attn_in_all, d_qkv).astype(BF16).reshape(nl, nb * share, 3 * local)
    qkv_part = lax.psum_scatter(qkv_term, "lat", scatter_dimension=0)
    qkv_part = lax.all_to_all(qkv_part.reshape(nb, share, 3 * local), "blk", 0, 0)
    qkv_grad = qkv_part.reshape(nb, share, 3, local).transpose(1, 2, 0, 3).reshape(share, 3 * width)
    qkv_grad = qkv_grad.astype(F32)

    grad_shift1 = jnp.sum(d_attn_in, axis=0, keepdims=True)
    grad_scale1 = jnp.sum(d_attn_in * normed1, axis=0, keepdims=True)
    grad_tokens = d_mid + norm_back(d_attn_in * (1.0 + scale1), normed1, rstd1)

    zero = jnp.zeros((width,), F32)
    bias_terms = [
        lax.dynamic_update_slice(zero, query_bias_term, (my_blk * local,)),
        lax.dynamic_update_slice(zero, value_bias_term, (my_blk * local,)),
        jnp.sum(d_proj, axis=0),
        jnp.sum(d_mlp, axis=0),
        jnp.sum(d_hidden, axis=0),
    ]
    bias_term = jnp.concatenate([term.reshape(n, -1) for term in bias_terms], axis=1)
    bias_grad = lax.psum_scatter(bias_term, BOTH, scatter_dimension=0)
    cuts = [share, 2 * share, 3 * share, 4 * share]
    q_grad, v_grad, out_grad, db_grad, ub_grad = jnp.split(bias_grad, cuts)

    d_mod = jnp.concatenate(
        [grad_shift1, grad_scale1, grad_gate1, grad_shift2, grad_scale2, grad_gate2], axis=1
    )
    d_mod = lax.all_gather(lax.psum(d_mod, "blk"), "lat", axis=0, tiled=True)
    ada_grad = lax.dot_general(picked, d_mod, (((0,), (0,)), ((), ())), precision=HIGH)
    mod_total = jnp.sum(d_mod, axis=0)
    ada_bias_grad = lax.dynamic_slice(mod_total, (index * ada_bias.shape[0],), ada_bias.shape)
    back_cond = lax.dot_general(
        d_mod, ada16.astype(F32), (((1,), (1,)), ((), ())), precision=HIGH
    )
    back_cond = lax.all_gather(back_cond, BOTH, axis=0)
    back_cond = lax.dynamic_index_in_dim(back_cond, my_lat, axis=1, keepdims=False)
    grad_condition = back_cond.reshape(1, width) * silu_slope(condition)
    return (
        output[None],
        grad_tokens[None],
        grad_condition,
        ada_grad,
        ada_bias_grad,
        qkv_grad,
        q_grad,
        v_grad,
        proj_grad,
        out_grad,
        up_grad,
        ub_grad,
        down_grad,
        db_grad,
    )


def solution(mesh):
    rows, vec = P(BOTH, None), P(BOTH)
    tok, cond = P("lat", "blk", None), P("lat", None)
    in_specs = (tok, cond, tok, rows, vec, rows, vec, vec, rows, vec, rows, vec, rows, vec)
    out_specs = (tok, tok, cond, rows, vec, rows, vec, vec, rows, vec, rows, vec, rows, vec)
    body = fused if mesh.shape["lat"] == 8 and mesh.shape["blk"] == 4 else generic
    return jax.shard_map(body, mesh=mesh, in_specs=in_specs, out_specs=out_specs, check_vma=False)
```

time: 2400 us -> 810 us (0.34)
  blocking collectives: 1390 us -> 133 us
  waiting for transfers between devices: 541 us -> 293 us
  Pallas kernels: 0 us -> 184 us
  local copies, waits for them, and re-layouts: 151 us -> 41.9 us
  starting transfers between devices: 109 us -> 18.5 us
  matrix products: 155 us -> 104 us
    unnamed x4 -> x1, blocking collectives: 1370 us -> 38.2 us
    all_gather x7 -> x0, waiting for transfers between devices: 400 us -> none  [the longest x1 109 us: per_device(): lax.all_gather(first_local[0], ('lat', 'blk'), axis=0, tiled=True)]
    pallas_call x0 -> x1, Pallas kernels: none -> 184 us  [forward(): pl.pallas_call(forward_kernel, out_shape=[shape for shape, _ in outs], in...]
    unnamed x211 -> x55, local copies, waits for them, and re-layouts: 137 us -> 4.72 us
    unnamed x20 -> x1, starting transfers between devices: 108 us -> 0.04 us
    reduce_scatter x4, waiting for transfers between devices: 140 us -> 241 us  [the longest x2 195 us: scatter_rows(): return lax.psum_scatter(pieces, BOTH, scatter_dimension=0).astype(F32)]
    all_gather x0 -> x2, blocking collectives: none -> 77.1 us  [the longest x1 67.7 us: fused(): back_cond = lax.all_gather(back_cond, BOTH, axis=0)]
    dot_general x20 -> x18, matrix products: 155 us -> 104 us  [the longest x4 27.1 us: dot_tn(): lax.dot_general(left, right, (((0,), (0,)), ((), ())), preferred_element_...]
  transfers between devices with their start and end apart: 31 -> 7, of which waited for: 9 -> 5; matrix products, arithmetic and copies ran while one was open for 61% -> 10% of each run, Pallas kernels for 0% -> 0%
where the time goes in v1:
time: 810 us; the launch traced here: 803 us
  waiting for transfers between devices  293 us (36%)
  Pallas kernels  184 us (23%)
  blocking collectives  133 us (16%)
  matrix products  104 us (13%)
  local copies, waits for them, and re-layouts  41.9 us (5%)
  starting transfers between devices  18.5 us (2%)
  between operations  14.5 us (2%)
  other arithmetic  13.8 us (2%)
    reduce_scatter x2, waiting for transfers between devices, scatter_rows(): return lax.psum_scatter(pieces, BOTH, scatter_dimension=0).astype(F32)  195 us
    pallas_call x1, Pallas kernels, forward(): pl.pallas_call(forward_kernel, out_shape=[shape for shape, _ in outs], in...  184 us
    all_gather x1, blocking collectives, fused(): back_cond = lax.all_gather(back_cond, BOTH, axis=0)  67.7 us
    reduce_scatter x1, waiting for transfers between devices, fused(): lax.psum_scatter(d_attn_in.astype(BF16).reshape(nb, rows, width), 'blk',...  45.8 us
    unnamed x6, waiting for transfers between devices  45.3 us
    unnamed x1, blocking collectives  38.2 us
    dot_general x4, matrix products, dot_tn(): lax.dot_general(left, right, (((0,), (0,)), ((), ())), preferred_element_...  27.1 us
    dot_general x4, matrix products, dot_nt(): lax.dot_general(left, right, (((1,), (1,)), ((), ())), preferred_element_...  23.7 us
  transfers between devices with their start and end apart: 7, of which 5 were waited for; matrix products, arithmetic and copies ran while one was open for 10% of the time, Pallas kernels for 0%

profile of v1, /device:TPU:0, one launch (start us, length us, event | category | flops | bytes accessed | tf_op | source)
XLA Modules:
  0.0 802.7 jit_solution(17951171558179442273)
XLA Ops:
  7.2 184.3 %forward.1 = (f32[1,16128]{1,0:T(1,128)}, f32[8,1,1152]{2,1,0:T(1,128)}, bf16[1152,4608]{1,0:T(8,128)(2,1)}, bf16[4608,1152]{1,0:T(8,128)(2,1)}, bf16[1152,1152]...) custom-call(f32[1,1152]{1,0:T(1,128)} %cond_ref.1, ...), custom_call_target="tpu_custom_call" | custom-call | tf_op jit(solution)/shard_map/forward/pallas_call | solution.py:496
  193.3 1.4 copy.63
  194.7 3.8 fusion.36
  198.8 6.3 convolution_add_fusion
  206.1 6.0 fusion.39
  212.1 9.2 %multiply_reduce_fusion.1 = (f32[1152]{0:T(1024)S(1)}, f32[256]{0:T(256)S(1)}, f32[256]{0:T(256)S(1)}, f32[1152]{0:T(1024)S(1)}, f32[256,1152]{1,0:T(8,128)}) fusion(f32[256,1152]{1,0:T(8,128)S(1)} %get-tuple-element.60, f32[256]{0:T(256)S(1)} %add_rsqrt_fusion.1, f32[256]{0:T(256)S(1)} %broadcast_multiply_fusion.5, f32[1152]{0:T(1024)S(1)} %get-tuple-element.54, ...), kind=kOutput, calls=%fused_computation.43 | convolution fusion | flops 2720560640 | bytes 15353344 | tf_op jit(solution)/shard_map/dot_general | solution.py:45
  221.3 8.0 fusion.24
  229.3 1.0 copy-done.7
  230.3 1.9 convolution_convert_fusion.5
  232.2 2.2 copy.66
  234.4 13.9 %all-to-all-start = ((bf16[4,4,256,72]{2,3,1,0:T(8,128)(2,1)}), bf16[4,4,256,72]{2,3,1,0:T(8,128)(2,1)}, u32[]{:S(2)}, u32[]{:S(2)}) async-start(bf16[4,4,256,72]{2,3,1,0:T(8,128)(2,1)} %bitcast.154), calls=%async_computation | async-start | bytes 1179648 | tf_op jit(solution)/shard_map/all_to_all | solution.py:588
  248.4 9.3 %fusion.40 = f32[4,1024,1024]{2,1,0:T(8,128)} fusion(bf16[4,1024,72]{2,1,0:T(8,128)(2,1)S(1)} %bitcast.146, bf16[4,1024,72]{2,1,0:T(8,128)(2,1)} %bitcast.148), kind=kOutput, calls=%fused_computation.107 | convolution fusion | flops 603979776 | bytes 17956864 | tf_op jit(solution)/shard_map/hqd,hkd->hqk/dot_general | solution.py:590
  257.6 7.3 all-to-all-done
  264.9 1.7 copy.67
  266.6 1.9 multiply_reduce_fusion
  268.5 8.5 %fusion.1 = f32[4,1024,72]{1,2,0:T(8,128)} fusion(bf16[4,1024,72]{2,1,0:T(8,128)(2,1)S(1)} %bitcast.143, f32[4,1024,1024]{2,1,0:T(8,128)} %fusion.40, f32[4,1024]{1,0:T(4,128)S(1)} %bitcast.163), kind=kOutput, calls=%fused_computation.5 | convolution fusion | flops 616562688 | bytes 18563072 | tf_op jit(solution)/shard_map/hqk,hqd->hkd/dot_general | solution.py:592
  277.0 8.9 %multiply_convert_fusion = bf16[4,1024,1024]{2,1,0:T(8,128)(2,1)S(1)} fusion(f32[4,1024,1024]{2,1,0:T(8,128)} %fusion.40, bf16[4,1024,72]{2,1,0:T(8,128)(2,1)S(1)} %bitcast.144, bf16[4,1024,72]{2,1,0:T(8,128)(2,1)} %bitcast.177, f32[4,1024]{1,0:T(4,128)S(1)} %bitcast.166, f32[4,1024]{1,0:T(4,128)S(1)} %bitcast.164), kind=kOutput, calls=%fused_computation.2 | convolution fusion | flops 629145600 | bytes 26378240 | tf_op jit(solution)/shard_map/hqd,hkd->hqk/dot_general | solution.py:593
  285.9 1.6 fusion.13
  287.5 2.8 fusion.37
  290.5 1.2 copy-done.12
  291.7 0.9 copy-done.18
  292.6 3.7 convolution_convert_fusion.4
  296.4 4.1 copy.74
  300.6 3.7 convolution_convert_fusion.2
  304.3 5.2 reshape.199
  309.8 6.6 convolution_convert_fusion.3
  317.1 10.9 %convolution_convert_fusion = bf16[4608,1152]{1,0:T(8,128)(2,1)} fusion(f32[1,256,1152]{2,1,0:T(8,128)} %param.16, f32[1152]{0:T(1024)S(1)} %copy-done.16, f32[256,4608]{1,0:T(8,128)} %copy-done.20), kind=kOutput, calls=%fused_computation | convolution fusion | flops 2734424064 | bytes 16519680 | tf_op jit(solution)/shard_map/dot_general | solution.py:49
  328.1 8.8 %convolution_convert_fusion.1 = bf16[1152,4608]{1,0:T(8,128)(2,1)} fusion(bf16[256,4608]{1,0:T(8,128)(2,1)} %copy-done.11, f32[256,1152]{1,0:T(8,128)S(1)} %get-tuple-element.60, f32[1152]{0:T(1024)S(1)} %get-tuple-element.53, f32[1152]{0:T(1024)S(1)} %get-tuple-element.54, f32[256]{0:T(256)S(1)} %add_rsqrt_fusion.1, f32[256]{0:T(256)S(1)} %broadcast_multiply_fusion.5), kind=kOutput, calls=%fused_computation.1 | convolution fusion | flops 2724691968 | bytes 14167040 | tf_op jit(solution)/shard_map/dot_general | solution.py:49
  336.8 13.9 %reshape.200 = bf16[32,36,4608]{2,1,0:T(8,128)(2,1)} reshape(bf16[1152,4608]{1,0:T(8,128)(2,1)} %convolution_convert_fusion.1) | data formatting | bytes 21233664 | tf_op jit(solution)/shard_map/reshape | solution.py:53
  352.9 38.2 %all-reduce = f32[32,288]{1,0:T(8,128)S(1)} all-reduce(f32[32,288]{1,0:T(8,128)S(1)} %concatenate.7), channel_id=5, replica_groups=mesh['lat'=8,'blk'=4] {'lat','blk'}, use_global_device_ids=true, to_apply=%region_24.0.clone | all-reduce | flops 9216 | bytes 73728
  392.4 1.7 reshape_reduce_scatter.3
  394.1 4.2 all-to-all-start.1
  398.3 45.2 %reduce-scatter.16.cloned.1.call-done = bf16[1,36,1152]{2,1,0:T(8,128)(2,1)} async-done(((bf16[32,36,1152]{2,1,0:T(8,128)(2,1)}), bf16[1,36,1152]{2,1,0:T(8,128)(2,1)}) %reduce-scatter.16.cloned.1.call-update) | async-done | bytes 82960
  443.5 1.6 bitcast_convert_fusion.2
  446.0 1.2 reshape.202
  447.1 45.8 %reduce-scatter.8.cloned.1.call-done = bf16[1,256,1152]{2,1,0:T(8,128)(2,1)} async-done(((bf16[4,256,1152]{2,1,0:T(8,128)(2,1)}), bf16[1,256,1152]{2,1,0:T(8,128)(2,1)}) %reduce-scatter.8.cloned.1.call-update) | async-done | bytes 589840 | tf_op jit(solution)/shard_map/reduce_scatter | solution.py:602
  492.9 1.2 convert_reduce_fusion
  494.0 1.6 fusion.19
  495.8 17.4 %psum.7 = f32[1,6912]{1,0:T(1,128)S(1)} all-reduce(f32[1,6912]{1,0:T(1,128)S(1)} %constant_dynamic-update-slice_fusion), channel_id=1, replica_groups=mesh['lat'=8,'blk'=4] {'blk'}, use_global_device_ids=true, to_apply=%region_16.0 | all-reduce | flops 6912 | bytes 55296 | tf_op jit(solution)/shard_map/psum | solution.py:631
  513.1 9.5 %all-gather.1 = f32[8,1,6912]{2,1,0:T(1,128)S(1)} all-gather(f32[1,1,6912]{2,1,0:T(1,128)S(1)} %bitcast.159), channel_id=1, replica_groups=mesh['lat'=8,'blk'=4] {'lat'}, dimensions={0}, use_global_device_ids=true | all-gather | bytes 248832 | tf_op jit(solution)/shard_map/all_gather | solution.py:631
  522.8 1.8 fusion.26
  524.6 67.7 %all-gather = f32[256,36]{1,0:T(8,128)S(1)} all-gather(f32[8,36]{1,0:T(8,128)S(1)} %fusion.26), channel_id=2, replica_groups=mesh['lat'=8,'blk'=4] {'lat','blk'}, dimensions={0}, use_global_device_ids=true | all-gather | bytes 38016 | tf_op jit(solution)/shard_map/all_gather | solution.py:638
  593.1 2.0 fusion.28
  595.7 1.5 fusion.17
  597.2 44.1 %reduce-scatter.14.cloned.1.call-done = bf16[1,144,1152]{2,1,0:T(8,128)(2,1)} async-done(((bf16[32,144,1152]{2,1,0:T(8,128)(2,1)}), bf16[1,144,1152]{2,1,0:T(8,128)(2,1)}) %reduce-scatter.14.cloned.1.call-update) | async-done | bytes 331792 | tf_op jit(solution)/shard_map/reduce_scatter | solution.py:54
  641.3 1.9 bitcast_convert_fusion.1
  643.1 150.9 %reduce-scatter.12.cloned.1.call-done = bf16[1,36,4608]{2,1,0:T(8,128)(2,1)} async-done(((bf16[32,36,4608]{2,1,0:T(8,128)(2,1)}), bf16[1,36,4608]{2,1,0:T(8,128)(2,1)}) %reduce-scatter.12.cloned.1.call-update) | async-done | bytes 331792 | tf_op jit(solution)/shard_map/reduce_scatter | solution.py:54
  794.0 1.9 bitcast_convert_fusion
  (103 shorter events, 10.1 us)
Async XLA Ops:
  7.2 186.0 %copy-start = (f32[1,256,1152]{2,1,0:T(8,128)S(1)}, f32[1,256,1152]{2,1,0:T(8,128)}, u32[]{:S(2)}) copy-start(f32[1,256,1152]{2,1,0:T(8,128)} %param.14) | copy-start | bytes 3538948
  193.2 28.2 %copy-start.15 = (f32[1152]{0:T(1024)}, f32[1152]{0:T(1024)S(1)}, u32[]{:S(2)}) copy-start(f32[1152]{0:T(1024)S(1)} %get-tuple-element.55) | copy-start | bytes 13828
  194.7 3.8 copy-start.5
  198.5 6.7 slice-start
  198.8 6.4 slice-start.1
  198.8 7.0 slice-start.2
  198.8 7.2 copy-start.19
  205.2 6.9 copy-start.20
  212.1 9.2 %copy-start.11 = (bf16[256,4608]{1,0:T(8,128)(2,1)}, bf16[256,4608]{1,0:T(8,128)(2,1)S(1)}, u32[]{:S(2)}) copy-start(bf16[256,4608]{1,0:T(8,128)(2,1)S(1)} %get-tuple-element.77) | copy-start | bytes 7077892
  221.3 9.0 %copy-start.10 = (bf16[1152,1152]{1,0:T(8,128)(2,1)S(1)}, bf16[1152,1152]{1,0:T(8,128)(2,1)}, u32[]{:S(2)}) copy-start(bf16[1152,1152]{1,0:T(8,128)(2,1)} %get-tuple-element.29) | copy-start | bytes 7962628
  229.3 1.0 copy-start.7
  232.2 16.1 %copy-start.14 = (f32[4,4,1,256]{3,2,1,0:T(1,128)S(1)}, f32[4,4,1,256]{3,2,1,0:T(1,128)}, u32[]{:S(2)}) copy-start(f32[4,4,1,256]{3,2,1,0:T(1,128)} %get-tuple-element.34) | copy-start | bytes 49156
  232.2 16.1 %copy-start.1 = (bf16[4,4,256,72]{3,2,1,0:T(8,128)(2,1)S(1)}, bf16[4,4,256,72]{3,2,1,0:T(8,128)(2,1)}, u32[]{:S(2)}) copy-start(bf16[4,4,256,72]{3,2,1,0:T(8,128)(2,1)} %get-tuple-element.32) | copy-start | bytes 1769476
  234.4 30.5 %all-to-all-start = ((bf16[4,4,256,72]{2,3,1,0:T(8,128)(2,1)}), bf16[4,4,256,72]{2,3,1,0:T(8,128)(2,1)}, u32[]{:S(2)}, u32[]{:S(2)}) async-start(bf16[4,4,256,72]{2,3,1,0:T(8,128)(2,1)} %bitcast.154), calls=%async_computation | async-start | bytes 1179648 | tf_op jit(solution)/shard_map/all_to_all | solution.py:588
  248.3 144.1 %reduce-scatter.10.cloned.1.call-start = ((), (), s32[]{:S(2)}) async-start(), calls=%async_computation.8 | async-start | bytes 2322432 | tf_op jit(solution)/shard_map/reduce_scatter | solution.py:606
  277.0 8.9 %copy-start.2 = (bf16[4,4,256,72]{3,2,1,0:T(8,128)(2,1)S(1)}, bf16[4,4,256,72]{3,2,1,0:T(8,128)(2,1)}, u32[]{:S(2)}) copy-start(bf16[4,4,256,72]{3,2,1,0:T(8,128)(2,1)} %get-tuple-element.32) | copy-start | bytes 1769476
  285.9 1.6 copy-start.3
  285.9 1.6 copy-start.9
  290.3 2.3 copy-start.18
  290.5 1.2 copy-start.12
  296.4 4.2 copy-start.6
  300.5 143.0 %reduce-scatter.16.cloned.1.call-start = ((), (), s32[]{:S(2)}) async-start(), calls=%async_computation.11 | async-start | bytes 3041280
  309.6 183.3 %reduce-scatter.8.cloned.1.call-start = ((), (), s32[]{:S(2)}) async-start(), calls=%async_computation.7 | async-start | bytes 2949120 | tf_op jit(solution)/shard_map/reduce_scatter | solution.py:602
  316.4 0.7 copy-start.16
  316.5 324.8 %reduce-scatter.14.cloned.1.call-start = ((), (), s32[]{:S(2)}) async-start(), calls=%async_computation.10 | async-start | bytes 10948608 | tf_op jit(solution)/shard_map/reduce_scatter | solution.py:54
  328.0 466.0 %reduce-scatter.12.cloned.1.call-start = ((), (), s32[]{:S(2)}) async-start(), calls=%async_computation.9 | async-start | bytes 12165120 | tf_op jit(solution)/shard_map/reduce_scatter | solution.py:54
  350.8 1.1 copy-start.17
  394.1 51.0 %all-to-all-start.1 = ((bf16[4,36,864]{2,1,0:T(8,128)(2,1)}), bf16[4,36,864]{2,1,0:T(8,128)(2,1)S(1)}, u32[]{:S(2)}, u32[]{:S(2)}) async-start(bf16[4,36,864]{2,1,0:T(8,128)(2,1)} %reshape_reduce_scatter.3), calls=%async_computation.3 | async-start | bytes 573440 | tf_op jit(solution)/shard_map/all_to_all | solution.py:607
  495.7 99.5 %copy-start.13 = (f32[1,1152]{1,0:T(1,128)S(1)}, f32[1,1152]{1,0:T(1,128)}, u32[]{:S(2)}) copy-start(f32[1,1152]{1,0:T(1,128)} %cond_ref.1) | copy-start | bytes 13828
  495.7 100.1 %copy-start.4 = (bf16[1,256,1152]{2,1,0:T(8,128)(2,1)S(1)}, bf16[1,256,1152]{2,1,0:T(8,128)(2,1)}, u32[]{:S(2)}) copy-start(bf16[1,256,1152]{2,1,0:T(8,128)(2,1)} %reduce-scatter.8.cloned.1.call-done) | copy-start | bytes 1769476
  495.7 100.1 %copy-start.8 = (f32[256,1152]{1,0:T(8,128)S(1)}, f32[256,1152]{1,0:T(8,128)}, u32[]{:S(2)}) copy-start(f32[256,1152]{1,0:T(8,128)} %copy-done.7) | copy-start | bytes 3538948
Sparse Core Ops, SparseCore 0:
  300.6 39.6 reduce-scatter.9
  346.6 96.8 reduce-scatter.15
  445.8 46.9 reduce-scatter.7
  498.8 142.4 reduce-scatter.13
  647.2 146.7 reduce-scatter.11
